TPU v7x, 256 devices: a whole 4x4x8 slice. The times are simulated.
256 devices in a mesh: dp: 64 (over z_lo, x, y, core), tp: 4 (over z_hi).
Axes of the slice: x: 4, y: 4, z: 8 (z_hi: 4, z_lo: 2; z = z_hi * 2 + z_lo), core: 2. Of those that a mesh axis runs over, the one named last changes fastest.
Arguments:
- tokens: bfloat16 [32768, 5120], P(('dp', 'tp')), may hold values from -24 to 24
- queries: bfloat16 [32768, 4096], P('dp', 'tp'), may hold values from -6 to 6
- grad_out: bfloat16 [32768, 4096], P('dp', 'tp'), may hold values from -6 to 6
- key_value_master_weight: float32 [2, 5120, 512], P(None, 'dp', 'tp'), may hold values from -6 to 6
- key_value_first_moment: float32 [2, 5120, 512], P(None, 'dp', 'tp'), may hold values from -6 to 6
- key_value_second_moment: float32 [2, 5120, 512], P(None, 'dp', 'tp'), may hold values from 0.5 to 8
- writer: int32 [64], replicated, may hold values from 0 to 63, each once
Outputs:
- grad_x: bfloat16 [32768, 5120], P(('dp', 'tp'))
- grad_q: bfloat16 [32768, 4096], P('dp', 'tp')
- new_master: float32 [2, 5120, 512], P(None, 'dp', 'tp')
- new_first: float32 [2, 5120, 512], P(None, 'dp', 'tp')
- new_second: float32 [2, 5120, 512], P(None, 'dp', 'tp')
- saved: bfloat16 [4096, 1280], P('dp', 'tp')
Inputs may be any that keep to these rules, and one draw needn't show every extreme that they name: writer is a permutation: each of the 64 replicas writes exactly one save shard.
All inputs are finite; a program needn't handle non-finite values.
Results may differ from a plain program's by a relative error of at most 0.017.
Values may be sent and summed in bfloat16 or wider, within the bound.
No kernel may reach another device: no remote copies, remote signals or barrier semaphores. Data moves between devices by JAX's collectives and lax.ppermute only.
A program may use at most 128 MiB of HBM per device.

v0:
```python
import functools
import math

import jax
import jax.numpy as jnp
from jax import lax
from jax.experimental import pallas as pl
from jax.experimental.pallas import tpu as pltpu
from jax.sharding import Mesh, PartitionSpec as P

HEAD_SIZE = 128


norm_eps = 1e-06
rope_base = 1000000.0
beta_one = 0.9
beta_two = 0.95
adam_eps = 1e-08
learn_rate = 0.02
weight_decay = 0.1
step_count = 10.0


def rope_tables(length, head_width):
    half_width = head_width // 2
    index_float = jnp.arange(half_width, dtype=jnp.float32)
    inverse_freq = rope_base ** (-2.0 * index_float / head_width)
    positions = jnp.arange(length, dtype=jnp.float32)
    angles = positions[:, None] * inverse_freq[None, :]
    return (jnp.cos(angles), jnp.sin(angles))


BF = jnp.bfloat16
F32 = jnp.float32
HALF = HEAD_SIZE // 2
PLACES = (0, -1, 1, 2)
NT = (((1,), (1,)), ((), ()))
TT = (((0,), (0,)), ((), ()))


def dot(left, right, dims=None):
    if dims is None:
        dims = (((1,), (0,)), ((), ()))
    return lax.dot_general(left, right, dims, preferred_element_type=F32)


def params(mebibytes=20):
    return pltpu.CompilerParams(vmem_limit_bytes=mebibytes * 1024 * 1024)


def norm_scale(field):
    return lax.rsqrt(jnp.mean(field * field, axis=-1, keepdims=True) + norm_eps)


def norm_back(field, factor, cotan):
    return factor * cotan - field * (factor * factor * factor) * jnp.mean(
        cotan * field, axis=-1, keepdims=True
    )


def turn(field, cosines, sines):
    return field * cosines + pltpu.roll(field, HALF, 1) * sines


def query_kernel(q_ref, cos_ref, sin_ref, out_ref):
    field = q_ref[...].astype(F32)
    out_ref[...] = turn(field * norm_scale(field), cos_ref[...], sin_ref[...]).astype(BF)


def rotated_queries(queries, cosines, sines):
    length, width = queries.shape
    column = pl.BlockSpec((length, HEAD_SIZE), lambda h: (0, h))
    table = pl.BlockSpec((length, HEAD_SIZE), lambda h: (0, 0))
    return pl.pallas_call(
        query_kernel,
        grid=(width // HEAD_SIZE,),
        in_specs=[column, table, table],
        out_specs=column,
        out_shape=jax.ShapeDtypeStruct(queries.shape, BF),
        compiler_params=params(),
        name="query_rope",
    )(queries, cosines, sines)


def row_loop(rows, step, body):
    def run(i, carry):
        body(pl.ds(pl.multiple_of(i * step, step), step))
        return carry

    lax.fori_loop(0, rows // step, run, 0)


def norm_kernel(in_ref, out_ref):
    def body(rows):
        field = in_ref[rows, :].astype(F32)
        out_ref[rows, :] = (field * norm_scale(field)).astype(BF)

    row_loop(in_ref.shape[0], 16, body)


def normed(tokens):
    block = pl.BlockSpec((tokens.shape[0] // 4, tokens.shape[1]), lambda i: (i, 0))
    return pl.pallas_call(
        norm_kernel,
        grid=(4,),
        in_specs=[block],
        out_specs=block,
        out_shape=jax.ShapeDtypeStruct(tokens.shape, BF),
        compiler_params=params(),
        name="norm",
    )(tokens)


def project_early_kernel(scale, offset_ref, first_ref, second_ref, *refs):
    w_refs, whole_ref, plain_ref = refs[:-2], refs[-2], refs[-1]
    block = whole_ref.shape[0] // offset_ref.shape[0]
    at = 0
    for w_ref in w_refs:
        count = w_ref.shape[0] // block

        def body(k, carry, at=at, w_ref=w_ref):
            row = pl.ds(pl.multiple_of(offset_ref[at + k], 16), block)
            whole_ref[row, :] = w_ref[pl.ds(pl.multiple_of(k * block, 16), block), :]
            return carry

        lax.fori_loop(0, count, body, 0)
        at += count
    plain_ref[...] = rows_times(first_ref, second_ref, whole_ref) * scale


def rows_times(first_ref, second_ref, whole_ref):
    chunk = whole_ref.shape[0] // 4
    total = 0.0
    for j in range(4):
        columns = slice(j * chunk, (j + 1) * chunk)
        field = jnp.concatenate([first_ref[:, columns], second_ref[:, columns]], axis=0)
        total = total + dot(field, whole_ref[columns])
    return total


def project_early(offsets, first, second, pieces, scale):
    vmem = pl.BlockSpec(memory_space=pltpu.VMEM)
    shape = (first.shape[1], pieces[0].shape[1])
    return pl.pallas_call(
        functools.partial(project_early_kernel, scale),
        in_specs=[pl.BlockSpec(memory_space=pltpu.SMEM)] + [vmem] * (2 + len(pieces)),
        out_specs=[vmem, vmem],
        out_shape=[
            jax.ShapeDtypeStruct(shape, BF),
            jax.ShapeDtypeStruct((2 * first.shape[0], shape[1]), F32),
        ],
        compiler_params=params(),
        name="project_early",
    )(offsets, first, second, *pieces)


def project_kernel(scale, order_ref, first_ref, second_ref, whole_ref, early_ref, cos_ref, sin_ref, plain_ref, *out_refs):
    tokens = cos_ref.shape[0]
    plain_ref[: 2 * tokens] = early_ref[...]
    plain_ref[2 * tokens :] = rows_times(first_ref, second_ref, whole_ref) * scale
    for k in range(4):
        rows = pl.ds(pl.multiple_of(order_ref[k] * tokens, tokens), tokens)
        u = plain_ref[rows, :HEAD_SIZE]
        out_refs[k][0] = turn(u * norm_scale(u), cos_ref[...], sin_ref[...]).astype(BF)
        out_refs[k][1] = plain_ref[rows, HEAD_SIZE:].astype(BF)


def project(order, first, second, weights, early, cosines, sines, scale):
    tokens = cosines.shape[0]
    vmem = pl.BlockSpec(memory_space=pltpu.VMEM)
    result = pl.pallas_call(
        functools.partial(project_kernel, scale),
        in_specs=[pl.BlockSpec(memory_space=pltpu.SMEM)] + [vmem] * 6,
        out_specs=[vmem] * 5,
        out_shape=[jax.ShapeDtypeStruct((4 * tokens, weights.shape[1]), F32)]
        + [jax.ShapeDtypeStruct((2, tokens, HEAD_SIZE), BF)] * 4,
        compiler_params=params(),
        name="project",
    )(order, first, second, weights, early, cosines, sines)
    return result[0], result[1:]


def sum_kernel(*refs):
    in_refs, out_refs = refs[:4], refs[4:]
    rows = out_refs[0].shape[0]
    for index, out_ref in enumerate(out_refs):
        part = slice(index * rows, (index + 1) * rows)
        total = sum(ref[part].astype(F32) for ref in in_refs[-3:]) + in_refs[0][part].astype(F32)
        out_ref[...] = total.astype(out_ref.dtype)


def sum_of(own, arrived, first_type):
    shape = (own.shape[0] // 4, own.shape[1])
    vmem = pl.BlockSpec(memory_space=pltpu.VMEM)
    return pl.pallas_call(
        sum_kernel,
        in_specs=[vmem] * 4,
        out_specs=[vmem] * 4,
        out_shape=[jax.ShapeDtypeStruct(shape, first_type)] + [jax.ShapeDtypeStruct(shape, BF)] * 3,
        compiler_params=params(),
        name="sum",
    )(own, *arrived)


def turn_kernel(offset_ref, first_ref, second_ref, out_ref, scratch):
    rows = first_ref.shape[0]
    block = scratch.shape[0] // offset_ref.shape[0]

    def turn_some(columns):
        scratch[columns, :rows] = first_ref[:, columns].T
        scratch[columns, rows:] = second_ref[:, columns].T

    row_loop(scratch.shape[0], 512, turn_some)

    def body(k, carry):
        row = pl.ds(pl.multiple_of(offset_ref[k], 16), block)
        out_ref[pl.ds(pl.multiple_of(k * block, 16), block), :] = scratch[row, :]
        return carry

    lax.fori_loop(0, offset_ref.shape[0], body, 0)


def turned(offsets, first, second):
    shape = (first.shape[1], 2 * first.shape[0])
    vmem = pl.BlockSpec(memory_space=pltpu.VMEM)
    return pl.pallas_call(
        turn_kernel,
        in_specs=[pl.BlockSpec(memory_space=pltpu.SMEM), vmem, vmem],
        out_specs=vmem,
        out_shape=jax.ShapeDtypeStruct(shape, BF),
        scratch_shapes=[pltpu.VMEM(shape, BF)],
        compiler_params=params(),
        name="turn",
    )(offsets, first, second)


def weight_grad_kernel(quarters, early_ref, late_ref, cotan_ref, *out_refs):
    rows = out_refs[0].shape[0]
    for index, out_ref in zip(quarters, out_refs):
        part = slice(index * rows, (index + 1) * rows)
        field = jnp.concatenate([early_ref[part], late_ref[part]], axis=1)
        out_ref[...] = dot(field, cotan_ref[...]).astype(BF)


def weight_grads(early, late, cotan, quarters):
    vmem = pl.BlockSpec(memory_space=pltpu.VMEM)
    shape = (early.shape[0] // 4, cotan.shape[1])
    return pl.pallas_call(
        functools.partial(weight_grad_kernel, quarters),
        in_specs=[vmem] * 3,
        out_specs=[vmem] * len(quarters),
        out_shape=[jax.ShapeDtypeStruct(shape, BF)] * len(quarters),
        compiler_params=params(),
        name="weight_grads",
    )(early, late, cotan)


def attention_kernel(order_ref, q_ref, g_ref, *refs):
    kv_refs, dkv_refs = refs[:4], refs[4:8]
    k_ref, ds0_ref, ds1_ref, v_ref, dk_acc, dv_acc = refs[8:]
    step = pl.program_id(0)
    length, width = q_ref.shape
    tokens, mid, heads = length // 4, length // 2, width // HEAD_SIZE
    scale = 1.0 / math.sqrt(HEAD_SIZE)

    @pl.when(step == 0)
    def _():
        dk_acc[...] = jnp.zeros_like(dk_acc)
        dv_acc[...] = jnp.zeros_like(dv_acc)
        for k in range(4):
            rows = pl.ds(pl.multiple_of(order_ref[k] * tokens, tokens), tokens)
            k_ref[rows, :] = kv_refs[k][0]
            v_ref[rows, :] = kv_refs[k][1]

    early, late = slice(0, mid), slice(mid, length)
    row = lax.broadcasted_iota(jnp.int32, (mid, mid), 0)
    column = lax.broadcasted_iota(jnp.int32, (mid, mid), 1)
    allowed = row <= column
    factor = scale * math.log2(math.e)
    each = range(heads)

    def at(ref, rows, h):
        return ref[rows, h * HEAD_SIZE : (h + 1) * HEAD_SIZE]

    def products(left_ref, right_ref):
        return [
            [
                dot(left_ref[early], at(right_ref, early, h), NT),
                dot(left_ref[early], at(right_ref, late, h), NT),
                dot(left_ref[late], at(right_ref, late, h), NT),
            ]
            for h in each
        ]

    def add(acc, terms, right_ref):
        acc[early] += sum(
            dot(terms[h][0], at(right_ref, early, h)) + dot(terms[h][1], at(right_ref, late, h))
            for h in each
        )
        acc[late] += sum(dot(terms[h][2], at(right_ref, late, h)) for h in each)

    def column_sums(terms):
        first, second, third = (jnp.sum(term, axis=0, keepdims=True) for term in terms)
        return first, second + third

    scores = products(k_ref, q_ref)
    d_probs = products(v_ref, g_ref)
    probs = []
    for h in each:
        a, b, c = scores[h]
        a = jnp.where(allowed, jnp.exp2(a * factor), 0.0)
        b = jnp.exp2(b * factor)
        c = jnp.where(allowed, jnp.exp2(c * factor), 0.0)
        sum_a, sum_b = column_sums((a, b, c))
        inv_a, inv_b = 1.0 / sum_a, 1.0 / sum_b
        probs.append((a * inv_a, b * inv_b, c * inv_b))
    add(dv_acc, [[term.astype(BF) for term in probs[h]] for h in each], g_ref)
    d_scores = []
    for h in each:
        sum_a, sum_b = column_sums([p * d for p, d in zip(probs[h], d_probs[h])])
        d_scores.append(
            [
                (p * (d - total)).astype(BF)
                for p, d, total in zip(probs[h], d_probs[h], (sum_a, sum_b, sum_b))
            ]
        )
        ds0_ref[h, :, :mid] = d_scores[h][0]
        ds0_ref[h, :, mid:] = d_scores[h][1]
        ds1_ref[h] = d_scores[h][2]
    add(dk_acc, d_scores, q_ref)

    @pl.when(step == pl.num_programs(0) - 1)
    def _():
        for k in range(4):
            rows = pl.ds(pl.multiple_of(order_ref[k] * tokens, tokens), tokens)
            dkv_refs[k][0] = (dk_acc[rows, :] * scale).astype(BF)
            dkv_refs[k][1] = dv_acc[rows, :].astype(BF)


def attention(order, rotated, incoming, pieces):
    length, width = rotated.shape
    heads, mid, pair = width // HEAD_SIZE, length // 2, 2
    columns = pl.BlockSpec((length, pair * HEAD_SIZE), lambda h: (0, h))
    whole = pl.BlockSpec((length, HEAD_SIZE), lambda h: (0, 0))
    piece = pl.BlockSpec(pieces[0].shape, lambda h: (0, 0, 0))
    result = pl.pallas_call(
        attention_kernel,
        grid=(heads // pair,),
        in_specs=[pl.BlockSpec(memory_space=pltpu.SMEM), columns, columns] + [piece] * 4,
        out_specs=[piece] * 4
        + [
            whole,
            pl.BlockSpec((pair, mid, length), lambda h: (h, 0, 0)),
            pl.BlockSpec((pair, mid, mid), lambda h: (h, 0, 0)),
        ],
        out_shape=[jax.ShapeDtypeStruct(pieces[0].shape, BF)] * 4
        + [
            jax.ShapeDtypeStruct((length, HEAD_SIZE), BF),
            jax.ShapeDtypeStruct((heads, mid, length), BF),
            jax.ShapeDtypeStruct((heads, mid, mid), BF),
        ],
        scratch_shapes=[pltpu.VMEM((length, HEAD_SIZE), BF)]
        + [pltpu.VMEM((length, HEAD_SIZE), F32)] * 2,
        compiler_params=params(32),
        name="attention",
    )(order, rotated, incoming, *pieces)
    return result[:4], result[4], result[5], result[6]


def grad_query_kernel(q_ref, k_ref, ds0_ref, ds1_ref, cos_ref, sin_ref, *refs):
    out_ref = refs[-1]
    mid = ds0_ref.shape[1]
    scale = 1.0 / math.sqrt(HEAD_SIZE)
    k0, k1 = k_ref[:mid], k_ref[mid:]
    both = dot(k0, ds0_ref[0], TT)
    early = both[:, :mid]
    late = both[:, mid:] + dot(k1, ds1_ref[0], TT)
    cotan = jnp.concatenate([early.T, late.T], axis=0) * scale
    field = q_ref[...].astype(F32)
    cotan = turn(cotan, cos_ref[...], -sin_ref[...])
    out_ref[...] = norm_back(field, norm_scale(field), cotan).astype(BF)


def grad_queries(queries, key, ds0, ds1, cosines, sines, first, given=None):
    length, width = queries.shape
    heads, mid = width // HEAD_SIZE, length // 2
    column = pl.BlockSpec((length, HEAD_SIZE), lambda h: (0, first + h))
    whole = pl.BlockSpec((length, HEAD_SIZE), lambda h: (0, 0))
    specs = [
        column,
        whole,
        pl.BlockSpec((1, mid, length), lambda h: (first + h, 0, 0)),
        pl.BlockSpec((1, mid, mid), lambda h: (first + h, 0, 0)),
        whole,
        whole,
    ]
    operands = [queries, key, ds0, ds1, cosines, sines]
    if given is not None:
        specs.append(pl.BlockSpec(memory_space=pl.ANY))
        operands.append(given)
    return pl.pallas_call(
        grad_query_kernel,
        grid=(heads // 2,),
        in_specs=specs,
        out_specs=column,
        out_shape=jax.ShapeDtypeStruct(queries.shape, BF),
        input_output_aliases={} if given is None else {6: 0},
        compiler_params=params(16),
        name="grad_query",
    )(*operands)


def cotan_kernel(order_ref, b0_ref, b1_ref, b2_ref, b3_ref, plain_ref, cos_ref, sin_ref, out_ref):
    tokens = cos_ref.shape[0]
    for k, back_ref in enumerate((b0_ref, b1_ref, b2_ref, b3_ref)):
        rows = pl.ds(pl.multiple_of(order_ref[k] * tokens, tokens), tokens)
        u = plain_ref[rows, :HEAD_SIZE]
        back = turn(back_ref[0].astype(F32), cos_ref[...], -sin_ref[...])
        out_ref[rows, :HEAD_SIZE] = norm_back(u, norm_scale(u), back).astype(BF)
        out_ref[rows, HEAD_SIZE:] = back_ref[1]


def key_value_cotan(order, back, plain, cosines, sines):
    vmem = pl.BlockSpec(memory_space=pltpu.VMEM)
    return pl.pallas_call(
        cotan_kernel,
        in_specs=[pl.BlockSpec(memory_space=pltpu.SMEM)] + [vmem] * 7,
        out_specs=vmem,
        out_shape=jax.ShapeDtypeStruct(plain.shape, BF),
        compiler_params=params(),
        name="key_value_cotan",
    )(order, *back, plain, cosines, sines)


def grad_token_kernel(x_ref, mine_ref, layer_ref, *refs):
    out_ref = refs[-1]

    def body(rows):
        cotan = mine_ref[rows, :].astype(F32) + layer_ref[rows, :].astype(F32)
        field = x_ref[rows, :].astype(F32)
        out_ref[rows, :] = norm_back(field, norm_scale(field), cotan).astype(BF)

    row_loop(x_ref.shape[0], 16, body)


def grad_tokens(tokens, mine, from_layer, start, given=None):
    step, width = from_layer.shape[0], tokens.shape[1]
    first = start // step
    here = pl.BlockSpec((step, width), lambda i: (first + i, 0))
    specs = [here, here, pl.BlockSpec((step, width), lambda i: (i, 0))]
    operands = [tokens, mine, from_layer]
    if given is not None:
        specs.append(pl.BlockSpec(memory_space=pl.ANY))
        operands.append(given)
    return pl.pallas_call(
        grad_token_kernel,
        grid=(from_layer.shape[0] // step,),
        in_specs=specs,
        out_specs=here,
        out_shape=jax.ShapeDtypeStruct(tokens.shape, BF),
        input_output_aliases={} if given is None else {3: 0},
        compiler_params=params(60),
        name="grad_tokens",
    )(*operands)


def plane_pairs(first, step):
    pairs = []
    for x in range(4):
        for y in range(4):
            for c in range(2):
                along_x = (c == 0) == first
                to_x = (x + step) % 4 if along_x else x
                to_y = y if along_x else (y + step) % 4
                pairs.append(((x * 4 + y) * 2 + c, (to_x * 4 + to_y) * 2 + c))
    return pairs


def far(block, step):
    return lax.ppermute(block, ("x", "y", "c"), plane_pairs(True, step))


def near(block, step):
    return lax.ppermute(block, ("x", "y", "c"), plane_pairs(False, step))


def swap_cores(block):
    return lax.ppermute(block, "c", [(0, 1), (1, 0)])


def group_pairs(target):
    pairs = []
    for g in range(4):
        for t in range(4):
            to_g, to_t = target(g, t)
            pairs.append((g * 4 + t, (to_g % 4) * 4 + to_t % 4))
    return pairs


def to_heads(block, k):
    return lax.ppermute(block, ("zl", "c", "t"), group_pairs(lambda g, t: (t, g + k)))


def from_heads(block, k):
    return lax.ppermute(block, ("zl", "c", "t"), group_pairs(lambda g, t: (t + k, g)))


def swap_layers(block):
    return lax.ppermute(block, "zl", [(0, 1), (1, 0)])


def after(first, *later):
    return lax.optimization_barrier((first,) + later)[1:]


def per_device(
    tokens,
    queries,
    grad_out,
    key_value_master_weight,
    key_value_first_moment,
    key_value_second_moment,
    writer,
):
    own_tokens, model_width = tokens.shape
    unit_scale = 1.0 / math.sqrt(model_width)
    length = queries.shape[0]
    rows = key_value_master_weight.shape[1]
    core = lax.axis_index("c")
    x_index, y_index = lax.axis_index("x"), lax.axis_index("y")
    t_index = lax.axis_index("t")
    g_index = 2 * lax.axis_index("zl") + core

    own_weight = key_value_master_weight.astype(BF)
    own_weight = jnp.concatenate([own_weight[0], own_weight[1]], axis=1)
    stage_parts = [to_heads(own_weight, k) for k in range(4)]
    stage = jnp.concatenate(stage_parts, axis=0)
    own_block = normed(tokens)
    from_z = swap_layers(after(stage_parts[0], own_block)[0])
    from_core = swap_cores(own_block)
    shard = jnp.concatenate([stage, near(stage, 1), near(stage, -1), near(stage, 2)], axis=0)
    pieces = [shard, far(shard, 1), far(shard, -1), far(shard, 2)]

    place = jnp.array(PLACES, jnp.int32)
    count = jnp.arange(4, dtype=jnp.int32)
    far_place = (jnp.where(core == 0, x_index, y_index) + place) % 4
    near_place = (jnp.where(core == 0, y_index, x_index) + place) % 4
    far_step = jnp.where(core == 0, 8 * rows, 2 * rows)
    near_step = jnp.where(core == 0, 2 * rows, 8 * rows)
    source = (t_index - count) % 4
    offsets = (
        far_place[:, None, None] * far_step
        + near_place[None, :, None] * near_step
        + ((source // 2) * (32 * rows) + (source % 2) * rows)[None, None, :]
    )
    offsets = offsets.reshape(64).astype(jnp.int32)
    sequence_order = ((t_index + count) % 4) ^ g_index
    block_order = (g_index - count) % 4

    cosines, sines = rope_tables(length, HEAD_SIZE)
    cosines = jnp.concatenate([cosines, cosines], axis=1)
    sines = jnp.concatenate([-sines, sines], axis=1)
    own_cos = lax.dynamic_slice_in_dim(cosines, t_index * own_tokens, own_tokens, 0)
    own_sin = lax.dynamic_slice_in_dim(sines, t_index * own_tokens, own_tokens, 0)
    rotated = rotated_queries(queries, cosines, sines)

    early = turned(offsets, own_block, from_core)
    from_core, from_z, own_cos, own_sin, sequence_order, block_order, offsets = after(
        (pieces, rotated, early), from_core, from_z, own_cos, own_sin, sequence_order, block_order, offsets
    )
    blocks = [own_block, from_core, from_z, swap_cores(from_z)]
    weights, plain_early = project_early(offsets, blocks[0], blocks[1], pieces, unit_scale)
    plain, projected = project(
        sequence_order, blocks[2], blocks[3], weights, plain_early, own_cos, own_sin, unit_scale
    )
    arrived = [from_heads(block, k) for k, block in enumerate(projected)]
    late = turned(offsets, *after(plain, blocks[2], blocks[3]))
    (arrived,) = after(late, arrived)

    returning, key, ds0, ds1 = attention(block_order, rotated, grad_out, arrived)
    back = [to_heads(block, -k) for k, block in enumerate(returning)]
    grad_q = grad_queries(queries, key, ds0, ds1, cosines, sines, 0)
    (back,) = after(grad_q, back)
    cotan = key_value_cotan(sequence_order, back, plain, own_cos, own_sin)

    part = [None] + list(weight_grads(early, late, cotan, (1, 2, 3)))
    arriving = [far(part[1], -1), far(part[2], 1), far(part[3], 2)]

    (cotan,) = after(part[1], cotan)
    rows_of = cotan.reshape(4, own_tokens, -1)
    sent = dot(jnp.concatenate([rows_of[1], rows_of[3]], axis=0), weights, NT) * unit_scale
    sent = sent.astype(BF)
    swapped = swap_cores(sent)
    (kept_from,) = after(sent, jnp.concatenate([rows_of[0], rows_of[2]], axis=0))
    kept = dot(kept_from, weights, NT) * unit_scale
    to_z = (kept[own_tokens:] + swapped[own_tokens:].astype(F32)).astype(BF)
    starts, cut = (96, 0, 48), (96, 48)
    to_z = [to_z[cut[0] :], to_z[: cut[1]], to_z[cut[1] : cut[0]]]
    z_first = swap_layers(to_z[0])

    kept, swapped, cotan = after(to_z, kept, swapped, cotan)
    part[0] = weight_grads(early, late, cotan, (0,))[0]
    mine = (kept[:own_tokens] + swapped[:own_tokens].astype(F32)).astype(BF)
    grad_x = grad_tokens(tokens, mine, z_first, starts[0])
    own_part, to_z[1], mine = after(grad_x, part[0], to_z[1], mine)
    own = sum_of(own_part, arriving, F32)
    z_second = swap_layers(to_z[1])
    summed = sum_of(own[0], [near(own[1], -1), near(own[2], 1), near(own[3], 2)], BF)
    grad_q = grad_queries(
        queries, key, after(own, ds0)[0], ds1, cosines, sines, queries.shape[1] // HEAD_SIZE // 2, grad_q
    )
    (summed,) = after((z_second, grad_q), summed)
    final = [from_heads(summed[k], -k) for k in range(4)]
    grad_x = grad_tokens(tokens, mine, after(summed, z_second)[0], starts[1], grad_x)
    (final,) = after(grad_x, final)
    final = sum(block.astype(F32) for block in final) * unit_scale
    weight_grad = jnp.stack([final[:, :HEAD_SIZE], final[:, HEAD_SIZE:]], axis=0)

    (to_z[2],) = after(final, to_z[2])
    grad_x = grad_tokens(tokens, mine, swap_layers(to_z[2]), starts[2], grad_x)

    new_first = beta_one * key_value_first_moment + (1.0 - beta_one) * weight_grad
    new_second = beta_two * key_value_second_moment + (1.0 - beta_two) * weight_grad * weight_grad
    first_hat = new_first / (1.0 - beta_one**step_count)
    second_hat = new_second / (1.0 - beta_two**step_count)
    new_master = key_value_master_weight - learn_rate * (
        first_hat / (jnp.sqrt(second_hat) + adam_eps) + weight_decay * key_value_master_weight
    )
    replicas = writer.shape[0]
    pieces = new_master.astype(BF).reshape(replicas, 2, -1)
    rank_ids = jnp.arange(replicas, dtype=jnp.int32)
    inverse = jnp.sum(jnp.where(writer[None, :] == rank_ids[:, None], rank_ids[None, :], 0), axis=1)
    outgoing = pieces.at[inverse].get(mode="promise_in_bounds")
    saved = lax.all_to_all(outgoing, ("zl", "x", "y", "c"), 0, 0, tiled=True)
    saved = after(grad_x, saved)[0].reshape(replicas, -1)
    return (grad_x, grad_q, new_master, new_first, new_second, saved)


def solution(mesh):
    fine = Mesh(mesh.devices.reshape(2, 4, 4, 2, 4), ("zl", "x", "y", "c", "t"))
    dp = ("zl", "x", "y", "c")
    every = dp + ("t",)
    weight = P(None, dp, "t")
    return jax.shard_map(
        per_device,
        mesh=fine,
        in_specs=(P(every, None), P(dp, "t"), P(dp, "t"), weight, weight, weight, P()),
        out_specs=(P(every, None), P(dp, "t"), weight, weight, weight, P(dp, "t")),
        check_vma=False,
    )
```

profile of v0, /device:TPU:1, one launch (start us, length us, event | category | flops | bytes accessed | tf_op | source)
XLA Modules:
  0.0 162.4 jit_solution(159698881336724522)
XLA Ops:
  1.6 6.3 %collective-permute-start.1 = (bf16[80,256]{1,0:T(8,128)(2,1)S(1)}, bf16[80,256]{1,0:T(8,128)(2,1)S(1)}, u32[]{:S(2)}, u32[]{:S(2)}) collective-permute-start(bf16[80,256]{1,0:T(8,128)(2,1)S(1)} %pad_maximum_fusion.4), channel_id=1, source_target_pairs={{0,0},{1,4},{2,128},{3,132},{4,1},{5,5},{6,129},{7,133},{128,2},{1... | collective-permute-start | bytes 122888 | tf_op jit(solution)/shard_map/ppermute | solution.py:501
  7.9 4.0 %collective-permute-start.2 = (bf16[80,256]{1,0:T(8,128)(2,1)S(1)}, bf16[80,256]{1,0:T(8,128)(2,1)S(1)}, u32[]{:S(2)}, u32[]{:S(2)}) collective-permute-start(bf16[80,256]{1,0:T(8,128)(2,1)S(1)} %pad_maximum_fusion.4), channel_id=1, source_target_pairs={{0,1},{1,5},{2,129},{3,133},{4,2},{5,6},{6,130},{7,134},{128,3},{1... | collective-permute-start | bytes 122888 | tf_op jit(solution)/shard_map/ppermute | solution.py:501
  11.9 3.3 %collective-permute-start.3 = (bf16[80,256]{1,0:T(8,128)(2,1)S(1)}, bf16[80,256]{1,0:T(8,128)(2,1)S(1)}, u32[]{:S(2)}, u32[]{:S(2)}) collective-permute-start(bf16[80,256]{1,0:T(8,128)(2,1)S(1)} %pad_maximum_fusion.4), channel_id=1, source_target_pairs={{0,2},{1,6},{2,130},{3,134},{4,3},{5,7},{6,131},{7,135},{128,0},{1... | collective-permute-start | bytes 122888 | tf_op jit(solution)/shard_map/ppermute | solution.py:501
  26.4 3.1 %collective-permute-done.7 = bf16[320,256]{1,0:T(8,128)(2,1)S(1)} collective-permute-done((bf16[320,256]{1,0:T(8,128)(2,1)S(1)}, bf16[320,256]{1,0:T(8,128)(2,1)S(1)}, u32[]{:S(2)}, u32[]{:S(2)}) %collective-permute-start.7) | collective-permute-done | bytes 163872 | tf_op jit(solution)/shard_map/ppermute | solution.py:484
  29.5 2.7 %collective-permute-start.10 = (bf16[1280,256]{1,0:T(8,128)(2,1)S(1)}, bf16[1280,256]{1,0:T(8,128)(2,1)S(1)}, u32[]{:S(2)}, u32[]{:S(2)}) collective-permute-start(bf16[1280,256]{1,0:T(8,128)(2,1)S(1)} %constant_dynamic-update-slice_fusion.4.refs_0_), channel_id=1, source_target_pairs={{0,64},{4,20},{8,72},{12,28},{16,80},{20,4},{24,88},{28,12},{32,96... | collective-permute-start | bytes 1966088 | tf_op jit(solution)/shard_map/ppermute | solution.py:480
  38.6 3.1 %turn.2.early_ref = bf16[5120,256]{1,0:T(8,128)(2,1)S(1)} custom-call(s32[64]{0:T(128)S(1)} %add.162.offset_ref, bf16[128,5120]{1,0:T(8,128)(2,1)S(1)} %norm.1.first_ref, bf16[128,5120]{1,0:T(8,128)(2,1)} %collective-permute-done.second_ref), custom_call_target="tpu_custom_call" | custom-call | tf_op jit(solution)/shard_map/turn/pallas_call | solution.py:226
  41.7 6.2 %collective-permute-done.8.refs_1_ = bf16[1280,256]{1,0:T(8,128)(2,1)S(1)} collective-permute-done((bf16[1280,256]{1,0:T(8,128)(2,1)S(1)}, bf16[1280,256]{1,0:T(8,128)(2,1)S(1)}, u32[]{:S(2)}, u32[]{:S(2)}) %collective-permute-start.8) | collective-permute-done | bytes 655392 | tf_op jit(solution)/shard_map/ppermute | solution.py:480
  51.7 2.7 %project_early.1 = (bf16[5120,256]{1,0:T(8,128)(2,1)S(1)}, f32[256,256]{1,0:T(8,128)S(1)}) custom-call(s32[64]{0:T(128)S(1)} %add.162.offset_ref, bf16[128,5120]{1,0:T(8,128)(2,1)S(1)} %norm.1.first_ref, bf16[128,5120]{1,0:T(8,128)(2,1)} %collective-permute-done.second_ref, bf16[1280,256]{1,0:T(8,128)(2,1)S(1)} %constant_dynamic-update-slice_fusion.4.refs_0_, ...), custom_call_target="tpu_custom_call" | custom-call | tf_op jit(solution)/shard_map/project_early/pallas_call | solution.py:144
  56.9 2.8 %collective-permute-start.13 = (bf16[2,128,128]{2,1,0:T(8,128)(2,1)S(1)}, bf16[2,128,128]{2,1,0:T(8,128)(2,1)S(1)}, u32[]{:S(2)}, u32[]{:S(2)}) collective-permute-start(bf16[2,128,128]{2,1,0:T(8,128)(2,1)S(1)} %get-tuple-element.82), channel_id=1, source_target_pairs={{0,0},{1,4},{2,128},{3,132},{4,1},{5,5},{6,129},{7,133},{128,2},{1... | collective-permute-start | bytes 196616 | tf_op jit(solution)/shard_map/ppermute | solution.py:505
  60.7 5.6 %collective-permute-start.16 = (bf16[2,128,128]{2,1,0:T(8,128)(2,1)S(1)}, bf16[2,128,128]{2,1,0:T(8,128)(2,1)S(1)}, u32[]{:S(2)}, u32[]{:S(2)}) collective-permute-start(bf16[2,128,128]{2,1,0:T(8,128)(2,1)S(1)} %get-tuple-element.85), channel_id=1, source_target_pairs={{0,132},{1,0},{2,4},{3,128},{4,133},{5,1},{6,5},{7,129},{128,134},... | collective-permute-start | bytes 196616 | tf_op jit(solution)/shard_map/ppermute | solution.py:505
  66.3 3.2 %turn.3.late_ref = bf16[5120,256]{1,0:T(8,128)(2,1)S(1)} custom-call(s32[64]{0:T(128)S(1)} %add.162.offset_ref, bf16[128,5120]{1,0:T(8,128)(2,1)} %collective-permute-done.11.first_ref, bf16[128,5120]{1,0:T(8,128)(2,1)S(1)} %collective-permute-done.12.second_ref), custom_call_target="tpu_custom_call" | custom-call | tf_op jit(solution)/shard_map/turn/pallas_call | solution.py:226
  69.5 5.9 %attention.1 = (bf16[2,128,128]{2,1,0:T(8,128)(2,1)S(1)}, bf16[2,128,128]{2,1,0:T(8,128)(2,1)S(1)}, bf16[2,128,128]{2,1,0:T(8,128)(2,1)S(1)}, bf16[2,128,128]{2,...) custom-call(s32[4]{0:T(128)S(1)} %get-tuple-element.81.order_ref, ...), custom_call_target="tpu_custom_call" | custom-call | tf_op jit(solution)/shard_map/attention/pallas_call | solution.py:346
  77.4 4.6 %collective-permute-start.19 = (bf16[2,128,128]{2,1,0:T(8,128)(2,1)S(1)}, bf16[2,128,128]{2,1,0:T(8,128)(2,1)S(1)}, u32[]{:S(2)}, u32[]{:S(2)}) collective-permute-start(bf16[2,128,128]{2,1,0:T(8,128)(2,1)S(1)} %get-tuple-element.95), channel_id=1, source_target_pairs={{0,2},{1,6},{2,130},{3,134},{4,3},{5,7},{6,131},{7,135},{128,0},{1... | collective-permute-start | bytes 196616 | tf_op jit(solution)/shard_map/ppermute | solution.py:501
  82.1 3.7 %collective-permute-start.20 = (bf16[2,128,128]{2,1,0:T(8,128)(2,1)S(1)}, bf16[2,128,128]{2,1,0:T(8,128)(2,1)S(1)}, u32[]{:S(2)}, u32[]{:S(2)}) collective-permute-start(bf16[2,128,128]{2,1,0:T(8,128)(2,1)S(1)} %get-tuple-element.96), channel_id=1, source_target_pairs={{0,1},{1,5},{2,129},{3,133},{4,2},{5,6},{6,130},{7,134},{128,3},{1... | collective-permute-start | bytes 196616 | tf_op jit(solution)/shard_map/ppermute | solution.py:501
  85.7 3.2 %grad_query.2.refs_0_ = bf16[512,1024]{1,0:T(8,128)(2,1)} custom-call(bf16[512,1024]{1,0:T(8,128)(2,1)S(1)} %copy-done.1, bf16[512,128]{1,0:T(8,128)(2,1)S(1)} %get-tuple-element.90.k_ref, bf16[8,256,512]{2,1,0:T(8,128)(2,1)S(1)} %get-tuple-element.116.ds0_ref, bf16[8,256,256]{2,1,0:T(8,128)(2,1)S(1)} %get-tuple-element.92.ds1_ref, ...), custom_call_target="tpu_custom_call" | custom-call | tf_op jit(solution)/shard_map/grad_query/pallas_call | solution.py:401
  100.7 3.0 %collective-permute-start.22 = (bf16[32,5120]{1,0:T(8,128)(2,1)S(1)}, bf16[32,5120]{1,0:T(8,128)(2,1)}, u32[]{:S(2)}, u32[]{:S(2)}) collective-permute-start(bf16[32,5120]{1,0:T(8,128)(2,1)S(1)} %slice.70), channel_id=1, source_target_pairs={{0,128},{128,0},{1,129},{129,1},{2,130},{130,2},{3,131},{131,3},{4... | collective-permute-start | bytes 983048 | tf_op jit(solution)/shard_map/ppermute | solution.py:509
  105.6 5.5 %collective-permute-done.22.layer_ref = bf16[32,5120]{1,0:T(8,128)(2,1)} collective-permute-done((bf16[32,5120]{1,0:T(8,128)(2,1)S(1)}, bf16[32,5120]{1,0:T(8,128)(2,1)}, u32[]{:S(2)}, u32[]{:S(2)}) %collective-permute-start.22) | collective-permute-done | bytes 327712 | tf_op jit(solution)/shard_map/ppermute | solution.py:509
  117.0 3.3 %collective-permute-start.27 = (bf16[320,256]{1,0:T(8,128)(2,1)S(1)}, bf16[320,256]{1,0:T(8,128)(2,1)S(1)}, u32[]{:S(2)}, u32[]{:S(2)}) collective-permute-start(bf16[320,256]{1,0:T(8,128)(2,1)S(1)} %get-tuple-element.113), channel_id=1, source_target_pairs={{0,24},{4,100},{8,0},{12,108},{16,8},{20,116},{24,16},{28,124},{32... | collective-permute-start | bytes 491528 | tf_op jit(solution)/shard_map/ppermute | solution.py:484
  123.7 3.2 %grad_query.3 = bf16[512,1024]{1,0:T(8,128)(2,1)} custom-call(bf16[512,1024]{1,0:T(8,128)(2,1)S(1)} %copy-done.1, bf16[512,128]{1,0:T(8,128)(2,1)S(1)} %get-tuple-element.90.k_ref, bf16[8,256,512]{2,1,0:T(8,128)(2,1)S(1)} %copy-done.3, bf16[8,256,256]{2,1,0:T(8,128)(2,1)S(1)} %get-tuple-element.92.ds1_ref, ...), custom_call_target="tpu_custom_call", output_to_operand_aliasing={{}: (6, {})} | custom-call | tf_op jit(solution)/shard_map/grad_query/pallas_call | solution.py:401
  127.8 6.5 %collective-permute-start.30 = (bf16[80,256]{1,0:T(8,128)(2,1)S(1)}, bf16[80,256]{1,0:T(8,128)(2,1)S(1)}, u32[]{:S(2)}, u32[]{:S(2)}) collective-permute-start(bf16[80,256]{1,0:T(8,128)(2,1)S(1)} %get-tuple-element.121), channel_id=1, source_target_pairs={{0,0},{1,4},{2,128},{3,132},{4,1},{5,5},{6,129},{7,133},{128,2},{1... | collective-permute-start | bytes 122888 | tf_op jit(solution)/shard_map/ppermute | solution.py:505
  135.7 3.6 %collective-permute-start.32 = (bf16[80,256]{1,0:T(8,128)(2,1)S(1)}, bf16[80,256]{1,0:T(8,128)(2,1)S(1)}, u32[]{:S(2)}, u32[]{:S(2)}) collective-permute-start(bf16[80,256]{1,0:T(8,128)(2,1)S(1)} %get-tuple-element.123), channel_id=1, source_target_pairs={{0,128},{1,132},{2,0},{3,4},{4,129},{5,133},{6,1},{7,5},{128,130},... | collective-permute-start | bytes 122888 | tf_op jit(solution)/shard_map/ppermute | solution.py:505
  139.3 2.8 %grad_tokens.4.refs_0_ = bf16[128,5120]{1,0:T(8,128)(2,1)} custom-call(bf16[128,5120]{1,0:T(8,128)(2,1)} %x_ref.5, bf16[128,5120]{1,0:T(8,128)(2,1)} %add_convert_fusion.mine_ref, bf16[48,5120]{1,0:T(8,128)(2,1)} %copy-done.6, bf16[128,5120]{1,0:T(8,128)(2,1)} %grad_tokens.3.refs_0_), custom_call_target="tpu_custom_call", output_to_operand_aliasing={{}: (3, {})} | custom-call | tf_op jit(solution)/shard_map/grad_tokens/pallas_call | solution.py:455
  147.9 5.6 %all-to-all-start = ((bf16[64,2,160]{2,1,0:T(2,128)(2,1)}), bf16[64,2,160]{2,1,0:T(2,128)(2,1)S(1)}, u32[]{:S(2)}, u32[]{:S(2)}) async-start(bf16[64,2,160]{2,1,0:T(2,128)(2,1)} %gather_fusion), calls=%async_computation | async-start | bytes 131072 | tf_op jit(solution)/shard_map/all_to_all | solution.py:634
  157.0 2.7 %grad_tokens.5 = bf16[128,5120]{1,0:T(8,128)(2,1)} custom-call(bf16[128,5120]{1,0:T(8,128)(2,1)} %x_ref.5, bf16[128,5120]{1,0:T(8,128)(2,1)} %add_convert_fusion.mine_ref, bf16[48,5120]{1,0:T(8,128)(2,1)} %copy-done.7, bf16[128,5120]{1,0:T(8,128)(2,1)} %grad_tokens.4.refs_0_), custom_call_target="tpu_custom_call", output_to_operand_aliasing={{}: (3, {})} | custom-call | tf_op jit(solution)/shard_map/grad_tokens/pallas_call | solution.py:455
  (127 shorter events, 64.7 us)
Async XLA Ops:
  1.6 18.8 %collective-permute-start.1 = (bf16[80,256]{1,0:T(8,128)(2,1)S(1)}, bf16[80,256]{1,0:T(8,128)(2,1)S(1)}, u32[]{:S(2)}, u32[]{:S(2)}) collective-permute-start(bf16[80,256]{1,0:T(8,128)(2,1)S(1)} %pad_maximum_fusion.4), channel_id=1, source_target_pairs={{0,0},{1,4},{2,128},{3,132},{4,1},{5,5},{6,129},{7,133},{128,2},{1... | collective-permute-start | bytes 122888 | tf_op jit(solution)/shard_map/ppermute | solution.py:501
  7.9 12.5 %collective-permute-start.2 = (bf16[80,256]{1,0:T(8,128)(2,1)S(1)}, bf16[80,256]{1,0:T(8,128)(2,1)S(1)}, u32[]{:S(2)}, u32[]{:S(2)}) collective-permute-start(bf16[80,256]{1,0:T(8,128)(2,1)S(1)} %pad_maximum_fusion.4), channel_id=1, source_target_pairs={{0,1},{1,5},{2,129},{3,133},{4,2},{5,6},{6,130},{7,134},{128,3},{1... | collective-permute-start | bytes 122888 | tf_op jit(solution)/shard_map/ppermute | solution.py:501
  11.9 8.6 %collective-permute-start.3 = (bf16[80,256]{1,0:T(8,128)(2,1)S(1)}, bf16[80,256]{1,0:T(8,128)(2,1)S(1)}, u32[]{:S(2)}, u32[]{:S(2)}) collective-permute-start(bf16[80,256]{1,0:T(8,128)(2,1)S(1)} %pad_maximum_fusion.4), channel_id=1, source_target_pairs={{0,2},{1,6},{2,130},{3,134},{4,3},{5,7},{6,131},{7,135},{128,0},{1... | collective-permute-start | bytes 122888 | tf_op jit(solution)/shard_map/ppermute | solution.py:501
  17.8 20.8 %collective-permute-start = (bf16[128,5120]{1,0:T(8,128)(2,1)S(1)}, bf16[128,5120]{1,0:T(8,128)(2,1)}, u32[]{:S(2)}, u32[]{:S(2)}) collective-permute-start(bf16[128,5120]{1,0:T(8,128)(2,1)S(1)} %norm.1.first_ref), channel_id=1, source_target_pairs={{0,4},{4,0},{1,5},{5,1},{2,6},{6,2},{3,7},{7,3},{8,12},{12,8},{9,1... | collective-permute-start | bytes 3932168 | tf_op jit(solution)/shard_map/ppermute | solution.py:488
  20.3 30.5 %collective-permute-start.11 = (bf16[128,5120]{1,0:T(8,128)(2,1)S(1)}, bf16[128,5120]{1,0:T(8,128)(2,1)}, u32[]{:S(2)}, u32[]{:S(2)}) collective-permute-start(bf16[128,5120]{1,0:T(8,128)(2,1)S(1)} %norm.1.first_ref), channel_id=1, source_target_pairs={{0,128},{128,0},{1,129},{129,1},{2,130},{130,2},{3,131},{131,3},{4... | collective-permute-start | bytes 3932168 | tf_op jit(solution)/shard_map/ppermute | solution.py:509
  29.5 12.2 %collective-permute-start.10 = (bf16[1280,256]{1,0:T(8,128)(2,1)S(1)}, bf16[1280,256]{1,0:T(8,128)(2,1)S(1)}, u32[]{:S(2)}, u32[]{:S(2)}) collective-permute-start(bf16[1280,256]{1,0:T(8,128)(2,1)S(1)} %constant_dynamic-update-slice_fusion.4.refs_0_), channel_id=1, source_target_pairs={{0,64},{4,20},{8,72},{12,28},{16,80},{20,4},{24,88},{28,12},{32,96... | collective-permute-start | bytes 1966088 | tf_op jit(solution)/shard_map/ppermute | solution.py:480
  32.2 15.6 %collective-permute-start.8 = (bf16[1280,256]{1,0:T(8,128)(2,1)S(1)}, bf16[1280,256]{1,0:T(8,128)(2,1)S(1)}, u32[]{:S(2)}, u32[]{:S(2)}) collective-permute-start(bf16[1280,256]{1,0:T(8,128)(2,1)S(1)} %constant_dynamic-update-slice_fusion.4.refs_0_), channel_id=1, source_target_pairs={{0,32},{4,12},{8,40},{12,20},{16,48},{20,28},{24,56},{28,4},{32,64... | collective-permute-start | bytes 1966088 | tf_op jit(solution)/shard_map/ppermute | solution.py:480
  32.7 15.4 %collective-permute-start.9 = (bf16[1280,256]{1,0:T(8,128)(2,1)S(1)}, bf16[1280,256]{1,0:T(8,128)(2,1)S(1)}, u32[]{:S(2)}, u32[]{:S(2)}) collective-permute-start(bf16[1280,256]{1,0:T(8,128)(2,1)S(1)} %constant_dynamic-update-slice_fusion.4.refs_0_), channel_id=1, source_target_pairs={{0,96},{4,28},{8,104},{12,4},{16,112},{20,12},{24,120},{28,20},{32... | collective-permute-start | bytes 1966088 | tf_op jit(solution)/shard_map/ppermute | solution.py:480
  56.9 12.5 %collective-permute-start.13 = (bf16[2,128,128]{2,1,0:T(8,128)(2,1)S(1)}, bf16[2,128,128]{2,1,0:T(8,128)(2,1)S(1)}, u32[]{:S(2)}, u32[]{:S(2)}) collective-permute-start(bf16[2,128,128]{2,1,0:T(8,128)(2,1)S(1)} %get-tuple-element.82), channel_id=1, source_target_pairs={{0,0},{1,4},{2,128},{3,132},{4,1},{5,5},{6,129},{7,133},{128,2},{1... | collective-permute-start | bytes 196616 | tf_op jit(solution)/shard_map/ppermute | solution.py:505
  59.8 9.7 %collective-permute-start.14 = (bf16[2,128,128]{2,1,0:T(8,128)(2,1)S(1)}, bf16[2,128,128]{2,1,0:T(8,128)(2,1)S(1)}, u32[]{:S(2)}, u32[]{:S(2)}) collective-permute-start(bf16[2,128,128]{2,1,0:T(8,128)(2,1)S(1)} %get-tuple-element.83), channel_id=1, source_target_pairs={{0,4},{1,128},{2,132},{3,0},{4,5},{5,129},{6,133},{7,1},{128,6},{1... | collective-permute-start | bytes 196616 | tf_op jit(solution)/shard_map/ppermute | solution.py:505
  60.0 9.4 %collective-permute-start.15 = (bf16[2,128,128]{2,1,0:T(8,128)(2,1)S(1)}, bf16[2,128,128]{2,1,0:T(8,128)(2,1)S(1)}, u32[]{:S(2)}, u32[]{:S(2)}) collective-permute-start(bf16[2,128,128]{2,1,0:T(8,128)(2,1)S(1)} %get-tuple-element.84), channel_id=1, source_target_pairs={{0,128},{1,132},{2,0},{3,4},{4,129},{5,133},{6,1},{7,5},{128,130},... | collective-permute-start | bytes 196616 | tf_op jit(solution)/shard_map/ppermute | solution.py:505
  60.7 8.8 %collective-permute-start.16 = (bf16[2,128,128]{2,1,0:T(8,128)(2,1)S(1)}, bf16[2,128,128]{2,1,0:T(8,128)(2,1)S(1)}, u32[]{:S(2)}, u32[]{:S(2)}) collective-permute-start(bf16[2,128,128]{2,1,0:T(8,128)(2,1)S(1)} %get-tuple-element.85), channel_id=1, source_target_pairs={{0,132},{1,0},{2,4},{3,128},{4,133},{5,1},{6,5},{7,129},{128,134},... | collective-permute-start | bytes 196616 | tf_op jit(solution)/shard_map/ppermute | solution.py:505
  75.4 13.6 %collective-permute-start.17 = (bf16[2,128,128]{2,1,0:T(8,128)(2,1)S(1)}, bf16[2,128,128]{2,1,0:T(8,128)(2,1)S(1)}, u32[]{:S(2)}, u32[]{:S(2)}) collective-permute-start(bf16[2,128,128]{2,1,0:T(8,128)(2,1)S(1)} %get-tuple-element.93), channel_id=1, source_target_pairs={{0,0},{1,4},{2,128},{3,132},{4,1},{5,5},{6,129},{7,133},{128,2},{1... | collective-permute-start | bytes 196616 | tf_op jit(solution)/shard_map/ppermute | solution.py:501
  77.3 11.6 %collective-permute-start.18 = (bf16[2,128,128]{2,1,0:T(8,128)(2,1)S(1)}, bf16[2,128,128]{2,1,0:T(8,128)(2,1)S(1)}, u32[]{:S(2)}, u32[]{:S(2)}) collective-permute-start(bf16[2,128,128]{2,1,0:T(8,128)(2,1)S(1)} %get-tuple-element.94), channel_id=1, source_target_pairs={{0,3},{1,7},{2,131},{3,135},{4,0},{5,4},{6,128},{7,132},{128,1},{1... | collective-permute-start | bytes 196616 | tf_op jit(solution)/shard_map/ppermute | solution.py:501
  77.4 11.5 %collective-permute-start.19 = (bf16[2,128,128]{2,1,0:T(8,128)(2,1)S(1)}, bf16[2,128,128]{2,1,0:T(8,128)(2,1)S(1)}, u32[]{:S(2)}, u32[]{:S(2)}) collective-permute-start(bf16[2,128,128]{2,1,0:T(8,128)(2,1)S(1)} %get-tuple-element.95), channel_id=1, source_target_pairs={{0,2},{1,6},{2,130},{3,134},{4,3},{5,7},{6,131},{7,135},{128,0},{1... | collective-permute-start | bytes 196616 | tf_op jit(solution)/shard_map/ppermute | solution.py:501
  94.4 20.3 %collective-permute-start.24 = (bf16[1280,256]{1,0:T(8,128)(2,1)}, bf16[1280,256]{1,0:T(8,128)(2,1)}, u32[]{:S(2)}, u32[]{:S(2)}) collective-permute-start(bf16[1280,256]{1,0:T(8,128)(2,1)} %get-tuple-element.101), channel_id=1, source_target_pairs={{0,96},{4,28},{8,104},{12,4},{16,112},{20,12},{24,120},{28,20},{32... | collective-permute-start | bytes 1966088 | tf_op jit(solution)/shard_map/ppermute | solution.py:480
  96.8 18.4 %collective-permute-start.25 = (bf16[1280,256]{1,0:T(8,128)(2,1)}, bf16[1280,256]{1,0:T(8,128)(2,1)}, u32[]{:S(2)}, u32[]{:S(2)}) collective-permute-start(bf16[1280,256]{1,0:T(8,128)(2,1)} %get-tuple-element.110), channel_id=1, source_target_pairs={{0,32},{4,12},{8,40},{12,20},{16,48},{20,28},{24,56},{28,4},{32,64... | collective-permute-start | bytes 1966088 | tf_op jit(solution)/shard_map/ppermute | solution.py:480
  96.9 18.3 %collective-permute-start.26 = (bf16[1280,256]{1,0:T(8,128)(2,1)}, bf16[1280,256]{1,0:T(8,128)(2,1)}, u32[]{:S(2)}, u32[]{:S(2)}) collective-permute-start(bf16[1280,256]{1,0:T(8,128)(2,1)} %get-tuple-element.111), channel_id=1, source_target_pairs={{0,64},{4,20},{8,72},{12,28},{16,80},{20,4},{24,88},{28,12},{32,96... | collective-permute-start | bytes 1966088 | tf_op jit(solution)/shard_map/ppermute | solution.py:480
  100.7 10.4 %collective-permute-start.22 = (bf16[32,5120]{1,0:T(8,128)(2,1)S(1)}, bf16[32,5120]{1,0:T(8,128)(2,1)}, u32[]{:S(2)}, u32[]{:S(2)}) collective-permute-start(bf16[32,5120]{1,0:T(8,128)(2,1)S(1)} %slice.70), channel_id=1, source_target_pairs={{0,128},{128,0},{1,129},{129,1},{2,130},{130,2},{3,131},{131,3},{4... | collective-permute-start | bytes 983048 | tf_op jit(solution)/shard_map/ppermute | solution.py:509
  113.4 14.4 %collective-permute-start.23 = (bf16[48,5120]{1,0:T(8,128)(2,1)S(1)}, bf16[48,5120]{1,0:T(8,128)(2,1)S(1)}, u32[]{:S(2)}, u32[]{:S(2)}) collective-permute-start(bf16[48,5120]{1,0:T(8,128)(2,1)S(1)} %get-tuple-element.108), channel_id=1, source_target_pairs={{0,128},{128,0},{1,129},{129,1},{2,130},{130,2},{3,131},{131,3},{4... | collective-permute-start | bytes 1474568 | tf_op jit(solution)/shard_map/ppermute | solution.py:509
  117.0 9.9 %collective-permute-start.27 = (bf16[320,256]{1,0:T(8,128)(2,1)S(1)}, bf16[320,256]{1,0:T(8,128)(2,1)S(1)}, u32[]{:S(2)}, u32[]{:S(2)}) collective-permute-start(bf16[320,256]{1,0:T(8,128)(2,1)S(1)} %get-tuple-element.113), channel_id=1, source_target_pairs={{0,24},{4,100},{8,0},{12,108},{16,8},{20,116},{24,16},{28,124},{32... | collective-permute-start | bytes 491528 | tf_op jit(solution)/shard_map/ppermute | solution.py:484
  127.8 14.3 %collective-permute-start.30 = (bf16[80,256]{1,0:T(8,128)(2,1)S(1)}, bf16[80,256]{1,0:T(8,128)(2,1)S(1)}, u32[]{:S(2)}, u32[]{:S(2)}) collective-permute-start(bf16[80,256]{1,0:T(8,128)(2,1)S(1)} %get-tuple-element.121), channel_id=1, source_target_pairs={{0,0},{1,4},{2,128},{3,132},{4,1},{5,5},{6,129},{7,133},{128,2},{1... | collective-permute-start | bytes 122888 | tf_op jit(solution)/shard_map/ppermute | solution.py:505
  143.1 13.1 %collective-permute-start.34 = (bf16[48,5120]{1,0:T(8,128)(2,1)S(1)}, bf16[48,5120]{1,0:T(8,128)(2,1)S(1)}, u32[]{:S(2)}, u32[]{:S(2)}) collective-permute-start(bf16[48,5120]{1,0:T(8,128)(2,1)S(1)} %copy-done.5), channel_id=1, source_target_pairs={{0,128},{128,0},{1,129},{129,1},{2,130},{130,2},{3,131},{131,3},{4... | collective-permute-start | bytes 1474568 | tf_op jit(solution)/shard_map/ppermute | solution.py:509
  147.9 13.8 %all-to-all-start = ((bf16[64,2,160]{2,1,0:T(2,128)(2,1)}), bf16[64,2,160]{2,1,0:T(2,128)(2,1)S(1)}, u32[]{:S(2)}, u32[]{:S(2)}) async-start(bf16[64,2,160]{2,1,0:T(2,128)(2,1)} %gather_fusion), calls=%async_computation | async-start | bytes 131072 | tf_op jit(solution)/shard_map/all_to_all | solution.py:634
  (25 other events, 175.8 us)
where the time goes:
time: 163 us; the launch traced here: 162 us
  starting transfers between devices  80.7 us (50%)
  Pallas kernels  40.7 us (25%)
  waiting for transfers between devices  26.2 us (16%)
  local copies, waits for them, and re-layouts  7.02 us (4%)
  other arithmetic  4.96 us (3%)
  matrix products  1.76 us (1%)
    ppermute x8, starting transfers between devices, to_heads(): lax.ppermute(block, ('zl', 'c', 't'), group_pairs(lambda g, t: (t, g + k)))  23.9 us
    ppermute x8, starting transfers between devices, from_heads(): lax.ppermute(block, ('zl', 'c', 't'), group_pairs(lambda g, t: (t + k, g)))  20.8 us
    ppermute x4, waiting for transfers between devices, swap_layers(): return lax.ppermute(block, 'zl', [(0, 1), (1, 0)])  10.9 us
    ppermute x6, starting transfers between devices, far(): return lax.ppermute(block, ('x', 'y', 'c'), plane_pairs(True, step))  9.53 us
    ppermute x6, starting transfers between devices, near(): return lax.ppermute(block, ('x', 'y', 'c'), plane_pairs(False, step))  9.44 us
    pallas_call x3, Pallas kernels, grad_tokens(): pl.pallas_call(grad_token_kernel, grid=(from_layer.shape[0] // step,), in...  7.88 us
    ppermute x6, waiting for transfers between devices, far(): return lax.ppermute(block, ('x', 'y', 'c'), plane_pairs(True, step))  7 us
    ppermute x4, starting transfers between devices, swap_layers(): return lax.ppermute(block, 'zl', [(0, 1), (1, 0)])  6.8 us
  transfers between devices with their start and end apart: 36, of which 14 were waited for; matrix products, arithmetic and copies ran while one was open for 5% of the time, Pallas kernels for 18%

commit v1 on v0

--- a/solution.py
+++ b/solution.py
@@ -410,7 +410,8 @@
     )(*operands)
 
 
-def cotan_kernel(order_ref, b0_ref, b1_ref, b2_ref, b3_ref, plain_ref, cos_ref, sin_ref, out_ref):
+def cotan_kernel(quarters, order_ref, b0_ref, b1_ref, b2_ref, b3_ref, plain_ref, cos_ref, sin_ref, *refs):
+    early_ref, late_ref, out_ref, part_refs = refs[0], refs[1], refs[2], refs[3:]
     tokens = cos_ref.shape[0]
     for k, back_ref in enumerate((b0_ref, b1_ref, b2_ref, b3_ref)):
         rows = pl.ds(pl.multiple_of(order_ref[k] * tokens, tokens), tokens)
@@ -418,18 +419,21 @@
         back = turn(back_ref[0].astype(F32), cos_ref[...], -sin_ref[...])
         out_ref[rows, :HEAD_SIZE] = norm_back(u, norm_scale(u), back).astype(BF)
         out_ref[rows, HEAD_SIZE:] = back_ref[1]
-
-
-def key_value_cotan(order, back, plain, cosines, sines):
+    weight_grad_kernel(quarters, early_ref, late_ref, out_ref, *part_refs)
+
+
+def key_value_cotan(order, back, plain, cosines, sines, early, late, quarters):
     vmem = pl.BlockSpec(memory_space=pltpu.VMEM)
-    return pl.pallas_call(
-        cotan_kernel,
-        in_specs=[pl.BlockSpec(memory_space=pltpu.SMEM)] + [vmem] * 7,
-        out_specs=vmem,
-        out_shape=jax.ShapeDtypeStruct(plain.shape, BF),
+    part = jax.ShapeDtypeStruct((early.shape[0] // 4, plain.shape[1]), BF)
+    result = pl.pallas_call(
+        functools.partial(cotan_kernel, quarters),
+        in_specs=[pl.BlockSpec(memory_space=pltpu.SMEM)] + [vmem] * 9,
+        out_specs=[vmem] * (1 + len(quarters)),
+        out_shape=[jax.ShapeDtypeStruct(plain.shape, BF)] + [part] * len(quarters),
         compiler_params=params(),
         name="key_value_cotan",
-    )(order, *back, plain, cosines, sines)
+    )(order, *back, plain, cosines, sines, early, late)
+    return result[0], result[1:]
 
 
 def grad_token_kernel(x_ref, mine_ref, layer_ref, *refs):
@@ -581,9 +585,11 @@
     back = [to_heads(block, -k) for k, block in enumerate(returning)]
     grad_q = grad_queries(queries, key, ds0, ds1, cosines, sines, 0)
     (back,) = after(grad_q, back)
-    cotan = key_value_cotan(sequence_order, back, plain, own_cos, own_sin)
-
-    part = [None] + list(weight_grads(early, late, cotan, (1, 2, 3)))
+    cotan, sent_parts = key_value_cotan(
+        sequence_order, back, plain, own_cos, own_sin, early, late, (1, 2, 3)
+    )
+
+    part = [None] + list(sent_parts)
     arriving = [far(part[1], -1), far(part[2], 1), far(part[3], 2)]
 
     (cotan,) = after(part[1], cotan)
@@ -594,15 +600,14 @@
     (kept_from,) = after(sent, jnp.concatenate([rows_of[0], rows_of[2]], axis=0))
     kept = dot(kept_from, weights, NT) * unit_scale
     to_z = (kept[own_tokens:] + swapped[own_tokens:].astype(F32)).astype(BF)
-    starts, cut = (96, 0, 48), (96, 48)
-    to_z = [to_z[cut[0] :], to_z[: cut[1]], to_z[cut[1] : cut[0]]]
+    starts = (0, 48, 96)
+    to_z = [to_z[starts[0] : starts[1]], to_z[starts[1] : starts[2]], to_z[starts[2] :]]
     z_first = swap_layers(to_z[0])
 
     kept, swapped, cotan = after(to_z, kept, swapped, cotan)
     part[0] = weight_grads(early, late, cotan, (0,))[0]
     mine = (kept[:own_tokens] + swapped[:own_tokens].astype(F32)).astype(BF)
-    grad_x = grad_tokens(tokens, mine, z_first, starts[0])
-    own_part, to_z[1], mine = after(grad_x, part[0], to_z[1], mine)
+    own_part, to_z[1] = after((z_first, mine), part[0], to_z[1])
     own = sum_of(own_part, arriving, F32)
     z_second = swap_layers(to_z[1])
     summed = sum_of(own[0], [near(own[1], -1), near(own[2], 1), near(own[3], 2)], BF)
@@ -611,12 +616,13 @@
     )
     (summed,) = after((z_second, grad_q), summed)
     final = [from_heads(summed[k], -k) for k in range(4)]
-    grad_x = grad_tokens(tokens, mine, after(summed, z_second)[0], starts[1], grad_x)
+    grad_x = grad_tokens(tokens, mine, after(summed, z_second)[0], starts[1])
     (final,) = after(grad_x, final)
     final = sum(block.astype(F32) for block in final) * unit_scale
     weight_grad = jnp.stack([final[:, :HEAD_SIZE], final[:, HEAD_SIZE:]], axis=0)
 
-    (to_z[2],) = after(final, to_z[2])
+    to_z[2], z_first = after(final, to_z[2], z_first)
+    grad_x = grad_tokens(tokens, mine, z_first, starts[0], grad_x)
     grad_x = grad_tokens(tokens, mine, swap_layers(to_z[2]), starts[2], grad_x)
 
     new_first = beta_one * key_value_first_moment + (1.0 - beta_one) * weight_grad

time: 163 us -> 162 us (level)
  waiting for transfers between devices: 26.2 us -> 29.6 us
  Pallas kernels: 40.7 us -> 38.1 us
  local copies, waits for them, and re-layouts: 7.02 us -> 4.52 us
    pallas_call x2 -> x1, Pallas kernels: 2.85 us -> 0.5 us  [weight_grads(): pl.pallas_call(functools.partial(weight_grad_kernel, quarters), in_specs=...]
    ppermute x6, starting transfers between devices: 9.53 us -> 7.74 us  [far(): return lax.ppermute(block, ('x', 'y', 'c'), plane_pairs(True, step))]
    unnamed x31 -> x27, local copies, waits for them, and re-layouts: 3.8 us -> 2.14 us
  transfers between devices with their start and end apart: 36 -> 36, of which waited for: 14 -> 13; matrix products, arithmetic and copies ran while one was open for 5% -> 4% of each run, Pallas kernels for 18% -> 17%
where the time goes in v1:
time: 162 us; the launch traced here: 161 us
  starting transfers between devices  80.9 us (50%)
  Pallas kernels  38.1 us (24%)
  waiting for transfers between devices  29.6 us (18%)
  other arithmetic  4.88 us (3%)
  local copies, waits for them, and re-layouts  4.52 us (3%)
  matrix products  1.76 us (1%)
    ppermute x8, starting transfers between devices, to_heads(): lax.ppermute(block, ('zl', 'c', 't'), group_pairs(lambda g, t: (t, g + k)))  23.9 us
    ppermute x8, starting transfers between devices, from_heads(): lax.ppermute(block, ('zl', 'c', 't'), group_pairs(lambda g, t: (t + k, g)))  21.1 us
    ppermute x4, waiting for transfers between devices, swap_layers(): return lax.ppermute(block, 'zl', [(0, 1), (1, 0)])  11.2 us
    ppermute x6, starting transfers between devices, near(): return lax.ppermute(block, ('x', 'y', 'c'), plane_pairs(False, step))  9.9 us
    ppermute x6, waiting for transfers between devices, far(): return lax.ppermute(block, ('x', 'y', 'c'), plane_pairs(True, step))  8.16 us
    pallas_call x3, Pallas kernels, grad_tokens(): pl.pallas_call(grad_token_kernel, grid=(from_layer.shape[0] // step,), in...  7.82 us
    ppermute x6, starting transfers between devices, far(): return lax.ppermute(block, ('x', 'y', 'c'), plane_pairs(True, step))  7.74 us
    all_to_all x1, starting transfers between devices, per_device(): saved = lax.all_to_all(outgoing, ('zl', 'x', 'y', 'c'), 0, 0, tiled=True)  6.98 us
  transfers between devices with their start and end apart: 36, of which 13 were waited for; matrix products, arithmetic and copies ran while one was open for 4% of the time, Pallas kernels for 17%

profile of v1, /device:TPU:1, one launch (start us, length us, event | category | flops | bytes accessed | tf_op | source)
XLA Modules:
  0.0 161.0 jit_solution(17557225188860950266)
XLA Ops:
  1.6 6.3 %collective-permute-start = (bf16[80,256]{1,0:T(8,128)(2,1)S(1)}, bf16[80,256]{1,0:T(8,128)(2,1)S(1)}, u32[]{:S(2)}, u32[]{:S(2)}) collective-permute-start(bf16[80,256]{1,0:T(8,128)(2,1)S(1)} %pad_maximum_fusion.4), channel_id=1, source_target_pairs={{0,0},{1,4},{2,128},{3,132},{4,1},{5,5},{6,129},{7,133},{128,2},{1... | collective-permute-start | bytes 122888 | tf_op jit(solution)/shard_map/ppermute | solution.py:505
  7.9 4.0 %collective-permute-start.1 = (bf16[80,256]{1,0:T(8,128)(2,1)S(1)}, bf16[80,256]{1,0:T(8,128)(2,1)S(1)}, u32[]{:S(2)}, u32[]{:S(2)}) collective-permute-start(bf16[80,256]{1,0:T(8,128)(2,1)S(1)} %pad_maximum_fusion.4), channel_id=1, source_target_pairs={{0,1},{1,5},{2,129},{3,133},{4,2},{5,6},{6,130},{7,134},{128,3},{1... | collective-permute-start | bytes 122888 | tf_op jit(solution)/shard_map/ppermute | solution.py:505
  11.9 3.3 %collective-permute-start.2 = (bf16[80,256]{1,0:T(8,128)(2,1)S(1)}, bf16[80,256]{1,0:T(8,128)(2,1)S(1)}, u32[]{:S(2)}, u32[]{:S(2)}) collective-permute-start(bf16[80,256]{1,0:T(8,128)(2,1)S(1)} %pad_maximum_fusion.4), channel_id=1, source_target_pairs={{0,2},{1,6},{2,130},{3,134},{4,3},{5,7},{6,131},{7,135},{128,0},{1... | collective-permute-start | bytes 122888 | tf_op jit(solution)/shard_map/ppermute | solution.py:505
  26.4 3.1 %collective-permute-done.6 = bf16[320,256]{1,0:T(8,128)(2,1)S(1)} collective-permute-done((bf16[320,256]{1,0:T(8,128)(2,1)S(1)}, bf16[320,256]{1,0:T(8,128)(2,1)S(1)}, u32[]{:S(2)}, u32[]{:S(2)}) %collective-permute-start.6) | collective-permute-done | bytes 163872 | tf_op jit(solution)/shard_map/ppermute | solution.py:488
  37.4 3.1 %turn.2.refs_0_.early_ref = bf16[5120,256]{1,0:T(8,128)(2,1)S(1)} custom-call(s32[64]{0:T(128)S(1)} %add.162.offset_ref, bf16[128,5120]{1,0:T(8,128)(2,1)S(1)} %norm.1.first_ref, bf16[128,5120]{1,0:T(8,128)(2,1)} %collective-permute-done.10.second_ref), custom_call_target="tpu_custom_call" | custom-call | tf_op jit(solution)/shard_map/turn/pallas_call | solution.py:226
  40.5 6.3 %collective-permute-done.8.refs_2_ = bf16[1280,256]{1,0:T(8,128)(2,1)S(1)} collective-permute-done((bf16[1280,256]{1,0:T(8,128)(2,1)S(1)}, bf16[1280,256]{1,0:T(8,128)(2,1)S(1)}, u32[]{:S(2)}, u32[]{:S(2)}) %collective-permute-start.8) | collective-permute-done | bytes 655392 | tf_op jit(solution)/shard_map/ppermute | solution.py:484
  51.7 2.7 %project_early.1 = (bf16[5120,256]{1,0:T(8,128)(2,1)S(1)}, f32[256,256]{1,0:T(8,128)S(1)}) custom-call(s32[64]{0:T(128)S(1)} %add.162.offset_ref, bf16[128,5120]{1,0:T(8,128)(2,1)S(1)} %norm.1.first_ref, bf16[128,5120]{1,0:T(8,128)(2,1)} %collective-permute-done.10.second_ref, bf16[1280,256]{1,0:T(8,128)(2,1)S(1)} %constant_dynamic-update-slice_fusion.4.refs_0_, ...), custom_call_target="tpu_custom_call" | custom-call | tf_op jit(solution)/shard_map/project_early/pallas_call | solution.py:144
  57.0 2.8 %collective-permute-start.13 = (bf16[2,128,128]{2,1,0:T(8,128)(2,1)S(1)}, bf16[2,128,128]{2,1,0:T(8,128)(2,1)S(1)}, u32[]{:S(2)}, u32[]{:S(2)}) collective-permute-start(bf16[2,128,128]{2,1,0:T(8,128)(2,1)S(1)} %get-tuple-element.83), channel_id=1, source_target_pairs={{0,0},{1,4},{2,128},{3,132},{4,1},{5,5},{6,129},{7,133},{128,2},{1... | collective-permute-start | bytes 196616 | tf_op jit(solution)/shard_map/ppermute | solution.py:509
  61.3 5.6 %collective-permute-start.16 = (bf16[2,128,128]{2,1,0:T(8,128)(2,1)S(1)}, bf16[2,128,128]{2,1,0:T(8,128)(2,1)S(1)}, u32[]{:S(2)}, u32[]{:S(2)}) collective-permute-start(bf16[2,128,128]{2,1,0:T(8,128)(2,1)S(1)} %get-tuple-element.86), channel_id=1, source_target_pairs={{0,132},{1,0},{2,4},{3,128},{4,133},{5,1},{6,5},{7,129},{128,134},... | collective-permute-start | bytes 196616 | tf_op jit(solution)/shard_map/ppermute | solution.py:509
  66.9 3.2 %turn.3.refs_1_.late_ref = bf16[5120,256]{1,0:T(8,128)(2,1)S(1)} custom-call(s32[64]{0:T(128)S(1)} %add.162.offset_ref, bf16[128,5120]{1,0:T(8,128)(2,1)} %collective-permute-done.11.first_ref, bf16[128,5120]{1,0:T(8,128)(2,1)S(1)} %collective-permute-done.12.second_ref), custom_call_target="tpu_custom_call" | custom-call | tf_op jit(solution)/shard_map/turn/pallas_call | solution.py:226
  70.1 5.9 %attention.1 = (bf16[2,128,128]{2,1,0:T(8,128)(2,1)S(1)}, bf16[2,128,128]{2,1,0:T(8,128)(2,1)S(1)}, bf16[2,128,128]{2,1,0:T(8,128)(2,1)S(1)}, bf16[2,128,128]{2,...) custom-call(s32[4]{0:T(128)S(1)} %get-tuple-element.72.order_ref, ...), custom_call_target="tpu_custom_call" | custom-call | tf_op jit(solution)/shard_map/attention/pallas_call | solution.py:346
  78.0 4.6 %collective-permute-start.19 = (bf16[2,128,128]{2,1,0:T(8,128)(2,1)S(1)}, bf16[2,128,128]{2,1,0:T(8,128)(2,1)S(1)}, u32[]{:S(2)}, u32[]{:S(2)}) collective-permute-start(bf16[2,128,128]{2,1,0:T(8,128)(2,1)S(1)} %get-tuple-element.96), channel_id=1, source_target_pairs={{0,2},{1,6},{2,130},{3,134},{4,3},{5,7},{6,131},{7,135},{128,0},{1... | collective-permute-start | bytes 196616 | tf_op jit(solution)/shard_map/ppermute | solution.py:505
  82.6 3.7 %collective-permute-start.20 = (bf16[2,128,128]{2,1,0:T(8,128)(2,1)S(1)}, bf16[2,128,128]{2,1,0:T(8,128)(2,1)S(1)}, u32[]{:S(2)}, u32[]{:S(2)}) collective-permute-start(bf16[2,128,128]{2,1,0:T(8,128)(2,1)S(1)} %get-tuple-element.97), channel_id=1, source_target_pairs={{0,1},{1,5},{2,129},{3,133},{4,2},{5,6},{6,130},{7,134},{128,3},{1... | collective-permute-start | bytes 196616 | tf_op jit(solution)/shard_map/ppermute | solution.py:505
  86.3 3.3 %grad_query.2.refs_0_ = bf16[512,1024]{1,0:T(8,128)(2,1)} custom-call(bf16[512,1024]{1,0:T(8,128)(2,1)S(1)} %copy-done.1, bf16[512,128]{1,0:T(8,128)(2,1)S(1)} %get-tuple-element.91.k_ref, bf16[8,256,512]{2,1,0:T(8,128)(2,1)S(1)} %get-tuple-element.117.ds0_ref, bf16[8,256,256]{2,1,0:T(8,128)(2,1)S(1)} %get-tuple-element.93.ds1_ref, ...), custom_call_target="tpu_custom_call" | custom-call | tf_op jit(solution)/shard_map/grad_query/pallas_call | solution.py:401
  98.7 2.9 %collective-permute-start.22 = (bf16[48,5120]{1,0:T(8,128)(2,1)S(1)}, bf16[48,5120]{1,0:T(8,128)(2,1)S(1)}, u32[]{:S(2)}, u32[]{:S(2)}) collective-permute-start(bf16[48,5120]{1,0:T(8,128)(2,1)S(1)} %get-tuple-element.139), channel_id=1, source_target_pairs={{0,128},{128,0},{1,129},{129,1},{2,130},{130,2},{3,131},{131,3},{4... | collective-permute-start | bytes 1474568 | tf_op jit(solution)/shard_map/ppermute | solution.py:513
  103.5 9.0 %collective-permute-done.22.layer_ref = bf16[48,5120]{1,0:T(8,128)(2,1)S(1)} collective-permute-done((bf16[48,5120]{1,0:T(8,128)(2,1)S(1)}, bf16[48,5120]{1,0:T(8,128)(2,1)S(1)}, u32[]{:S(2)}, u32[]{:S(2)}) %collective-permute-start.22) | collective-permute-done | bytes 491552 | tf_op jit(solution)/shard_map/ppermute | solution.py:513
  114.1 3.6 %collective-permute-start.27 = (bf16[320,256]{1,0:T(8,128)(2,1)S(1)}, bf16[320,256]{1,0:T(8,128)(2,1)S(1)}, u32[]{:S(2)}, u32[]{:S(2)}) collective-permute-start(bf16[320,256]{1,0:T(8,128)(2,1)S(1)} %get-tuple-element.114), channel_id=1, source_target_pairs={{0,24},{4,100},{8,0},{12,108},{16,8},{20,116},{24,16},{28,124},{32... | collective-permute-start | bytes 491528 | tf_op jit(solution)/shard_map/ppermute | solution.py:488
  119.6 3.3 %grad_query.3 = bf16[512,1024]{1,0:T(8,128)(2,1)} custom-call(bf16[512,1024]{1,0:T(8,128)(2,1)S(1)} %copy-done.1, bf16[512,128]{1,0:T(8,128)(2,1)S(1)} %get-tuple-element.91.k_ref, bf16[8,256,512]{2,1,0:T(8,128)(2,1)S(1)} %get-tuple-element.117.ds0_ref, bf16[8,256,256]{2,1,0:T(8,128)(2,1)S(1)} %get-tuple-element.93.ds1_ref, ...), custom_call_target="tpu_custom_call", output_to_operand_aliasing={{}: (6, {})} | custom-call | tf_op jit(solution)/shard_map/grad_query/pallas_call | solution.py:401
  125.2 6.3 %collective-permute-start.30 = (bf16[80,256]{1,0:T(8,128)(2,1)S(1)}, bf16[80,256]{1,0:T(8,128)(2,1)S(1)}, u32[]{:S(2)}, u32[]{:S(2)}) collective-permute-start(bf16[80,256]{1,0:T(8,128)(2,1)S(1)} %get-tuple-element.122), channel_id=1, source_target_pairs={{0,0},{1,4},{2,128},{3,132},{4,1},{5,5},{6,129},{7,133},{128,2},{1... | collective-permute-start | bytes 122888 | tf_op jit(solution)/shard_map/ppermute | solution.py:509
  132.9 3.6 %collective-permute-start.32 = (bf16[80,256]{1,0:T(8,128)(2,1)S(1)}, bf16[80,256]{1,0:T(8,128)(2,1)S(1)}, u32[]{:S(2)}, u32[]{:S(2)}) collective-permute-start(bf16[80,256]{1,0:T(8,128)(2,1)S(1)} %get-tuple-element.124), channel_id=1, source_target_pairs={{0,128},{1,132},{2,0},{3,4},{4,129},{5,133},{6,1},{7,5},{128,130},... | collective-permute-start | bytes 122888 | tf_op jit(solution)/shard_map/ppermute | solution.py:509
  136.5 2.7 %grad_tokens.3.refs_0_ = bf16[128,5120]{1,0:T(8,128)(2,1)} custom-call(bf16[128,5120]{1,0:T(8,128)(2,1)} %x_ref.5, bf16[128,5120]{1,0:T(8,128)(2,1)} %add_convert_fusion.mine_ref, bf16[48,5120]{1,0:T(8,128)(2,1)} %copy-done.3), custom_call_target="tpu_custom_call" | custom-call | tf_op jit(solution)/shard_map/grad_tokens/pallas_call | solution.py:459
  140.2 2.6 %collective-permute-start.34 = (bf16[32,5120]{1,0:T(8,128)(2,1)S(1)}, bf16[32,5120]{1,0:T(8,128)(2,1)S(1)}, u32[]{:S(2)}, u32[]{:S(2)}) collective-permute-start(bf16[32,5120]{1,0:T(8,128)(2,1)S(1)} %slice.72), channel_id=1, source_target_pairs={{0,128},{128,0},{1,129},{129,1},{2,130},{130,2},{3,131},{131,3},{4... | collective-permute-start | bytes 983048 | tf_op jit(solution)/shard_map/ppermute | solution.py:513
  145.1 7.0 %all-to-all-start = ((bf16[64,2,160]{2,1,0:T(2,128)(2,1)}), bf16[64,2,160]{2,1,0:T(2,128)(2,1)S(1)}, u32[]{:S(2)}, u32[]{:S(2)}) async-start(bf16[64,2,160]{2,1,0:T(2,128)(2,1)} %gather_fusion), calls=%async_computation | async-start | bytes 131072 | tf_op jit(solution)/shard_map/all_to_all | solution.py:640
  152.1 2.8 %grad_tokens.4.refs_0_ = bf16[128,5120]{1,0:T(8,128)(2,1)} custom-call(bf16[128,5120]{1,0:T(8,128)(2,1)} %x_ref.5, bf16[128,5120]{1,0:T(8,128)(2,1)} %add_convert_fusion.mine_ref, bf16[48,5120]{1,0:T(8,128)(2,1)} %copy-done.4, bf16[128,5120]{1,0:T(8,128)(2,1)} %grad_tokens.3.refs_0_), custom_call_target="tpu_custom_call", output_to_operand_aliasing={{}: (3, {})} | custom-call | tf_op jit(solution)/shard_map/grad_tokens/pallas_call | solution.py:459
  (122 shorter events, 58.2 us)
Async XLA Ops:
  1.6 18.8 %collective-permute-start = (bf16[80,256]{1,0:T(8,128)(2,1)S(1)}, bf16[80,256]{1,0:T(8,128)(2,1)S(1)}, u32[]{:S(2)}, u32[]{:S(2)}) collective-permute-start(bf16[80,256]{1,0:T(8,128)(2,1)S(1)} %pad_maximum_fusion.4), channel_id=1, source_target_pairs={{0,0},{1,4},{2,128},{3,132},{4,1},{5,5},{6,129},{7,133},{128,2},{1... | collective-permute-start | bytes 122888 | tf_op jit(solution)/shard_map/ppermute | solution.py:505
  7.9 12.5 %collective-permute-start.1 = (bf16[80,256]{1,0:T(8,128)(2,1)S(1)}, bf16[80,256]{1,0:T(8,128)(2,1)S(1)}, u32[]{:S(2)}, u32[]{:S(2)}) collective-permute-start(bf16[80,256]{1,0:T(8,128)(2,1)S(1)} %pad_maximum_fusion.4), channel_id=1, source_target_pairs={{0,1},{1,5},{2,129},{3,133},{4,2},{5,6},{6,130},{7,134},{128,3},{1... | collective-permute-start | bytes 122888 | tf_op jit(solution)/shard_map/ppermute | solution.py:505
  11.9 8.6 %collective-permute-start.2 = (bf16[80,256]{1,0:T(8,128)(2,1)S(1)}, bf16[80,256]{1,0:T(8,128)(2,1)S(1)}, u32[]{:S(2)}, u32[]{:S(2)}) collective-permute-start(bf16[80,256]{1,0:T(8,128)(2,1)S(1)} %pad_maximum_fusion.4), channel_id=1, source_target_pairs={{0,2},{1,6},{2,130},{3,134},{4,3},{5,7},{6,131},{7,135},{128,0},{1... | collective-permute-start | bytes 122888 | tf_op jit(solution)/shard_map/ppermute | solution.py:505
  17.8 19.6 %collective-permute-start.10 = (bf16[128,5120]{1,0:T(8,128)(2,1)S(1)}, bf16[128,5120]{1,0:T(8,128)(2,1)}, u32[]{:S(2)}, u32[]{:S(2)}) collective-permute-start(bf16[128,5120]{1,0:T(8,128)(2,1)S(1)} %norm.1.first_ref), channel_id=1, source_target_pairs={{0,4},{4,0},{1,5},{5,1},{2,6},{6,2},{3,7},{7,3},{8,12},{12,8},{9,1... | collective-permute-start | bytes 3932168 | tf_op jit(solution)/shard_map/ppermute | solution.py:492
  20.3 30.5 %collective-permute-start.11 = (bf16[128,5120]{1,0:T(8,128)(2,1)S(1)}, bf16[128,5120]{1,0:T(8,128)(2,1)}, u32[]{:S(2)}, u32[]{:S(2)}) collective-permute-start(bf16[128,5120]{1,0:T(8,128)(2,1)S(1)} %norm.1.first_ref), channel_id=1, source_target_pairs={{0,128},{128,0},{1,129},{129,1},{2,130},{130,2},{3,131},{131,3},{4... | collective-permute-start | bytes 3932168 | tf_op jit(solution)/shard_map/ppermute | solution.py:513
  29.5 11.0 %collective-permute-start.7 = (bf16[1280,256]{1,0:T(8,128)(2,1)S(1)}, bf16[1280,256]{1,0:T(8,128)(2,1)S(1)}, u32[]{:S(2)}, u32[]{:S(2)}) collective-permute-start(bf16[1280,256]{1,0:T(8,128)(2,1)S(1)} %constant_dynamic-update-slice_fusion.4.refs_0_), channel_id=1, source_target_pairs={{0,32},{4,12},{8,40},{12,20},{16,48},{20,28},{24,56},{28,4},{32,64... | collective-permute-start | bytes 1966088 | tf_op jit(solution)/shard_map/ppermute | solution.py:484
  30.6 16.2 %collective-permute-start.8 = (bf16[1280,256]{1,0:T(8,128)(2,1)S(1)}, bf16[1280,256]{1,0:T(8,128)(2,1)S(1)}, u32[]{:S(2)}, u32[]{:S(2)}) collective-permute-start(bf16[1280,256]{1,0:T(8,128)(2,1)S(1)} %constant_dynamic-update-slice_fusion.4.refs_0_), channel_id=1, source_target_pairs={{0,96},{4,28},{8,104},{12,4},{16,112},{20,12},{24,120},{28,20},{32... | collective-permute-start | bytes 1966088 | tf_op jit(solution)/shard_map/ppermute | solution.py:484
  32.2 16.4 %collective-permute-start.9 = (bf16[1280,256]{1,0:T(8,128)(2,1)S(1)}, bf16[1280,256]{1,0:T(8,128)(2,1)S(1)}, u32[]{:S(2)}, u32[]{:S(2)}) collective-permute-start(bf16[1280,256]{1,0:T(8,128)(2,1)S(1)} %constant_dynamic-update-slice_fusion.4.refs_0_), channel_id=1, source_target_pairs={{0,64},{4,20},{8,72},{12,28},{16,80},{20,4},{24,88},{28,12},{32,96... | collective-permute-start | bytes 1966088 | tf_op jit(solution)/shard_map/ppermute | solution.py:484
  57.0 13.1 %collective-permute-start.13 = (bf16[2,128,128]{2,1,0:T(8,128)(2,1)S(1)}, bf16[2,128,128]{2,1,0:T(8,128)(2,1)S(1)}, u32[]{:S(2)}, u32[]{:S(2)}) collective-permute-start(bf16[2,128,128]{2,1,0:T(8,128)(2,1)S(1)} %get-tuple-element.83), channel_id=1, source_target_pairs={{0,0},{1,4},{2,128},{3,132},{4,1},{5,5},{6,129},{7,133},{128,2},{1... | collective-permute-start | bytes 196616 | tf_op jit(solution)/shard_map/ppermute | solution.py:509
  59.8 10.3 %collective-permute-start.14 = (bf16[2,128,128]{2,1,0:T(8,128)(2,1)S(1)}, bf16[2,128,128]{2,1,0:T(8,128)(2,1)S(1)}, u32[]{:S(2)}, u32[]{:S(2)}) collective-permute-start(bf16[2,128,128]{2,1,0:T(8,128)(2,1)S(1)} %get-tuple-element.84), channel_id=1, source_target_pairs={{0,4},{1,128},{2,132},{3,0},{4,5},{5,129},{6,133},{7,1},{128,6},{1... | collective-permute-start | bytes 196616 | tf_op jit(solution)/shard_map/ppermute | solution.py:509
  60.1 10.0 %collective-permute-start.15 = (bf16[2,128,128]{2,1,0:T(8,128)(2,1)S(1)}, bf16[2,128,128]{2,1,0:T(8,128)(2,1)S(1)}, u32[]{:S(2)}, u32[]{:S(2)}) collective-permute-start(bf16[2,128,128]{2,1,0:T(8,128)(2,1)S(1)} %get-tuple-element.85), channel_id=1, source_target_pairs={{0,128},{1,132},{2,0},{3,4},{4,129},{5,133},{6,1},{7,5},{128,130},... | collective-permute-start | bytes 196616 | tf_op jit(solution)/shard_map/ppermute | solution.py:509
  61.3 8.8 %collective-permute-start.16 = (bf16[2,128,128]{2,1,0:T(8,128)(2,1)S(1)}, bf16[2,128,128]{2,1,0:T(8,128)(2,1)S(1)}, u32[]{:S(2)}, u32[]{:S(2)}) collective-permute-start(bf16[2,128,128]{2,1,0:T(8,128)(2,1)S(1)} %get-tuple-element.86), channel_id=1, source_target_pairs={{0,132},{1,0},{2,4},{3,128},{4,133},{5,1},{6,5},{7,129},{128,134},... | collective-permute-start | bytes 196616 | tf_op jit(solution)/shard_map/ppermute | solution.py:509
  76.0 13.6 %collective-permute-start.17 = (bf16[2,128,128]{2,1,0:T(8,128)(2,1)S(1)}, bf16[2,128,128]{2,1,0:T(8,128)(2,1)S(1)}, u32[]{:S(2)}, u32[]{:S(2)}) collective-permute-start(bf16[2,128,128]{2,1,0:T(8,128)(2,1)S(1)} %get-tuple-element.94), channel_id=1, source_target_pairs={{0,0},{1,4},{2,128},{3,132},{4,1},{5,5},{6,129},{7,133},{128,2},{1... | collective-permute-start | bytes 196616 | tf_op jit(solution)/shard_map/ppermute | solution.py:505
  77.9 11.7 %collective-permute-start.18 = (bf16[2,128,128]{2,1,0:T(8,128)(2,1)S(1)}, bf16[2,128,128]{2,1,0:T(8,128)(2,1)S(1)}, u32[]{:S(2)}, u32[]{:S(2)}) collective-permute-start(bf16[2,128,128]{2,1,0:T(8,128)(2,1)S(1)} %get-tuple-element.95), channel_id=1, source_target_pairs={{0,3},{1,7},{2,131},{3,135},{4,0},{5,4},{6,128},{7,132},{128,1},{1... | collective-permute-start | bytes 196616 | tf_op jit(solution)/shard_map/ppermute | solution.py:505
  78.0 11.6 %collective-permute-start.19 = (bf16[2,128,128]{2,1,0:T(8,128)(2,1)S(1)}, bf16[2,128,128]{2,1,0:T(8,128)(2,1)S(1)}, u32[]{:S(2)}, u32[]{:S(2)}) collective-permute-start(bf16[2,128,128]{2,1,0:T(8,128)(2,1)S(1)} %get-tuple-element.96), channel_id=1, source_target_pairs={{0,2},{1,6},{2,130},{3,134},{4,3},{5,7},{6,131},{7,135},{128,0},{1... | collective-permute-start | bytes 196616 | tf_op jit(solution)/shard_map/ppermute | solution.py:505
  93.8 19.9 %collective-permute-start.24 = (bf16[1280,256]{1,0:T(8,128)(2,1)S(1)}, bf16[1280,256]{1,0:T(8,128)(2,1)S(1)}, u32[]{:S(2)}, u32[]{:S(2)}) collective-permute-start(bf16[1280,256]{1,0:T(8,128)(2,1)S(1)} %get-tuple-element.102), channel_id=1, source_target_pairs={{0,96},{4,28},{8,104},{12,4},{16,112},{20,12},{24,120},{28,20},{32... | collective-permute-start | bytes 1966088 | tf_op jit(solution)/shard_map/ppermute | solution.py:484
  95.6 18.1 %collective-permute-start.25 = (bf16[1280,256]{1,0:T(8,128)(2,1)S(1)}, bf16[1280,256]{1,0:T(8,128)(2,1)S(1)}, u32[]{:S(2)}, u32[]{:S(2)}) collective-permute-start(bf16[1280,256]{1,0:T(8,128)(2,1)S(1)} %get-tuple-element.111), channel_id=1, source_target_pairs={{0,32},{4,12},{8,40},{12,20},{16,48},{20,28},{24,56},{28,4},{32,64... | collective-permute-start | bytes 1966088 | tf_op jit(solution)/shard_map/ppermute | solution.py:484
  95.7 18.0 %collective-permute-start.26 = (bf16[1280,256]{1,0:T(8,128)(2,1)S(1)}, bf16[1280,256]{1,0:T(8,128)(2,1)S(1)}, u32[]{:S(2)}, u32[]{:S(2)}) collective-permute-start(bf16[1280,256]{1,0:T(8,128)(2,1)S(1)} %get-tuple-element.112), channel_id=1, source_target_pairs={{0,64},{4,20},{8,72},{12,28},{16,80},{20,4},{24,88},{28,12},{32,96... | collective-permute-start | bytes 1966088 | tf_op jit(solution)/shard_map/ppermute | solution.py:484
  98.7 13.8 %collective-permute-start.22 = (bf16[48,5120]{1,0:T(8,128)(2,1)S(1)}, bf16[48,5120]{1,0:T(8,128)(2,1)S(1)}, u32[]{:S(2)}, u32[]{:S(2)}) collective-permute-start(bf16[48,5120]{1,0:T(8,128)(2,1)S(1)} %get-tuple-element.139), channel_id=1, source_target_pairs={{0,128},{128,0},{1,129},{129,1},{2,130},{130,2},{3,131},{131,3},{4... | collective-permute-start | bytes 1474568 | tf_op jit(solution)/shard_map/ppermute | solution.py:513
  112.5 12.7 %collective-permute-start.23 = (bf16[48,5120]{1,0:T(8,128)(2,1)S(1)}, bf16[48,5120]{1,0:T(8,128)(2,1)S(1)}, u32[]{:S(2)}, u32[]{:S(2)}) collective-permute-start(bf16[48,5120]{1,0:T(8,128)(2,1)S(1)} %get-tuple-element.109), channel_id=1, source_target_pairs={{0,128},{128,0},{1,129},{129,1},{2,130},{130,2},{3,131},{131,3},{4... | collective-permute-start | bytes 1474568 | tf_op jit(solution)/shard_map/ppermute | solution.py:513
  114.1 8.8 %collective-permute-start.27 = (bf16[320,256]{1,0:T(8,128)(2,1)S(1)}, bf16[320,256]{1,0:T(8,128)(2,1)S(1)}, u32[]{:S(2)}, u32[]{:S(2)}) collective-permute-start(bf16[320,256]{1,0:T(8,128)(2,1)S(1)} %get-tuple-element.114), channel_id=1, source_target_pairs={{0,24},{4,100},{8,0},{12,108},{16,8},{20,116},{24,16},{28,124},{32... | collective-permute-start | bytes 491528 | tf_op jit(solution)/shard_map/ppermute | solution.py:488
  125.2 14.0 %collective-permute-start.30 = (bf16[80,256]{1,0:T(8,128)(2,1)S(1)}, bf16[80,256]{1,0:T(8,128)(2,1)S(1)}, u32[]{:S(2)}, u32[]{:S(2)}) collective-permute-start(bf16[80,256]{1,0:T(8,128)(2,1)S(1)} %get-tuple-element.122), channel_id=1, source_target_pairs={{0,0},{1,4},{2,128},{3,132},{4,1},{5,5},{6,129},{7,133},{128,2},{1... | collective-permute-start | bytes 122888 | tf_op jit(solution)/shard_map/ppermute | solution.py:509
  140.2 14.6 %collective-permute-start.34 = (bf16[32,5120]{1,0:T(8,128)(2,1)S(1)}, bf16[32,5120]{1,0:T(8,128)(2,1)S(1)}, u32[]{:S(2)}, u32[]{:S(2)}) collective-permute-start(bf16[32,5120]{1,0:T(8,128)(2,1)S(1)} %slice.72), channel_id=1, source_target_pairs={{0,128},{128,0},{1,129},{129,1},{2,130},{130,2},{3,131},{131,3},{4... | collective-permute-start | bytes 983048 | tf_op jit(solution)/shard_map/ppermute | solution.py:513
  145.1 15.2 %all-to-all-start = ((bf16[64,2,160]{2,1,0:T(2,128)(2,1)}), bf16[64,2,160]{2,1,0:T(2,128)(2,1)S(1)}, u32[]{:S(2)}, u32[]{:S(2)}) async-start(bf16[64,2,160]{2,1,0:T(2,128)(2,1)} %gather_fusion), calls=%async_computation | async-start | bytes 131072 | tf_op jit(solution)/shard_map/all_to_all | solution.py:640
  (23 other events, 200.7 us)

commit v2 on v1

--- a/solution.py
+++ b/solution.py
@@ -635,8 +635,8 @@
     replicas = writer.shape[0]
     pieces = new_master.astype(BF).reshape(replicas, 2, -1)
     rank_ids = jnp.arange(replicas, dtype=jnp.int32)
-    inverse = jnp.sum(jnp.where(writer[None, :] == rank_ids[:, None], rank_ids[None, :], 0), axis=1)
-    outgoing = pieces.at[inverse].get(mode="promise_in_bounds")
+    chosen = (writer[None, :] == rank_ids[:, None]).astype(BF)
+    outgoing = dot(chosen, pieces).astype(BF)
     saved = lax.all_to_all(outgoing, ("zl", "x", "y", "c"), 0, 0, tiled=True)
     saved = after(grad_x, saved)[0].reshape(replicas, -1)
     return (grad_x, grad_q, new_master, new_first, new_second, saved)

time: 162 us -> 162 us (level)
    ppermute x4, starting transfers between devices: 6.78 us -> 11.9 us  [swap_layers(): return lax.ppermute(block, 'zl', [(0, 1), (1, 0)])]
    ppermute x4, waiting for transfers between devices: 11.2 us -> 8.5 us  [swap_layers(): return lax.ppermute(block, 'zl', [(0, 1), (1, 0)])]
    ppermute x8, starting transfers between devices: 23.9 us -> 21.9 us  [to_heads(): lax.ppermute(block, ('zl', 'c', 't'), group_pairs(lambda g, t: (t, g + k)))]
    ppermute x3, starting transfers between devices: 4.52 us -> 2.6 us  [swap_cores(): return lax.ppermute(block, 'c', [(0, 1), (1, 0)])]
  transfers between devices with their start and end apart: 36 -> 36, of which waited for: 13 -> 10; matrix products, arithmetic and copies ran while one was open for 4% -> 4% of each run, Pallas kernels for 17% -> 17%
where the time goes in v2:
time: 162 us; the launch traced here: 161 us
  starting transfers between devices  81.3 us (50%)
  Pallas kernels  38.1 us (24%)
  waiting for transfers between devices  30 us (19%)
  other arithmetic  4.75 us (3%)
  local copies, waits for them, and re-layouts  3.9 us (2%)
  matrix products  1.91 us (1%)
    ppermute x8, starting transfers between devices, to_heads(): lax.ppermute(block, ('zl', 'c', 't'), group_pairs(lambda g, t: (t, g + k)))  21.9 us
    ppermute x8, starting transfers between devices, from_heads(): lax.ppermute(block, ('zl', 'c', 't'), group_pairs(lambda g, t: (t + k, g)))  21.3 us
    ppermute x4, starting transfers between devices, swap_layers(): return lax.ppermute(block, 'zl', [(0, 1), (1, 0)])  11.9 us
    ppermute x6, starting transfers between devices, near(): return lax.ppermute(block, ('x', 'y', 'c'), plane_pairs(False, step))  9.3 us
    ppermute x4, waiting for transfers between devices, swap_layers(): return lax.ppermute(block, 'zl', [(0, 1), (1, 0)])  8.5 us
    ppermute x6, waiting for transfers between devices, near(): return lax.ppermute(block, ('x', 'y', 'c'), plane_pairs(False, step))  7.87 us
    pallas_call x3, Pallas kernels, grad_tokens(): pl.pallas_call(grad_token_kernel, grid=(from_layer.shape[0] // step,), in...  7.82 us
    all_to_all x1, starting transfers between devices, per_device(): saved = lax.all_to_all(outgoing, ('zl', 'x', 'y', 'c'), 0, 0, tiled=True)  7.47 us
  transfers between devices with their start and end apart: 36, of which 10 were waited for; matrix products, arithmetic and copies ran while one was open for 4% of the time, Pallas kernels for 17%

profile of v2, /device:TPU:1, one launch (start us, length us, event | category | flops | bytes accessed | tf_op | source)
XLA Modules:
  0.0 161.2 jit_solution(13762140030077402632)
XLA Ops:
  1.6 3.3 %collective-permute-start.3 = (bf16[80,256]{1,0:T(8,128)(2,1)S(1)}, bf16[80,256]{1,0:T(8,128)(2,1)S(1)}, u32[]{:S(2)}, u32[]{:S(2)}) collective-permute-start(bf16[80,256]{1,0:T(8,128)(2,1)S(1)} %pad_maximum_fusion.4), channel_id=1, source_target_pairs={{0,3},{1,7},{2,131},{3,135},{4,0},{5,4},{6,128},{7,132},{128,1},{1... | collective-permute-start | bytes 122888 | tf_op jit(solution)/shard_map/ppermute | solution.py:505
  4.9 4.6 %collective-permute-start.2 = (bf16[80,256]{1,0:T(8,128)(2,1)S(1)}, bf16[80,256]{1,0:T(8,128)(2,1)S(1)}, u32[]{:S(2)}, u32[]{:S(2)}) collective-permute-start(bf16[80,256]{1,0:T(8,128)(2,1)S(1)} %pad_maximum_fusion.4), channel_id=1, source_target_pairs={{0,2},{1,6},{2,130},{3,134},{4,3},{5,7},{6,131},{7,135},{128,0},{1... | collective-permute-start | bytes 122888 | tf_op jit(solution)/shard_map/ppermute | solution.py:505
  18.1 3.8 %collective-permute-start.11 = (bf16[128,5120]{1,0:T(8,128)(2,1)S(1)}, bf16[128,5120]{1,0:T(8,128)(2,1)}, u32[]{:S(2)}, u32[]{:S(2)}) collective-permute-start(bf16[128,5120]{1,0:T(8,128)(2,1)S(1)} %norm.1.first_ref), channel_id=1, source_target_pairs={{0,128},{128,0},{1,129},{129,1},{2,130},{130,2},{3,131},{131,3},{4... | collective-permute-start | bytes 3932168 | tf_op jit(solution)/shard_map/ppermute | solution.py:513
  26.6 5.4 %collective-permute-done.4 = bf16[320,256]{1,0:T(8,128)(2,1)S(1)} collective-permute-done((bf16[320,256]{1,0:T(8,128)(2,1)S(1)}, bf16[320,256]{1,0:T(8,128)(2,1)S(1)}, u32[]{:S(2)}, u32[]{:S(2)}) %collective-permute-start.4) | collective-permute-done | bytes 163872 | tf_op jit(solution)/shard_map/ppermute | solution.py:488
  32.1 2.7 %collective-permute-start.9 = (bf16[1280,256]{1,0:T(8,128)(2,1)S(1)}, bf16[1280,256]{1,0:T(8,128)(2,1)S(1)}, u32[]{:S(2)}, u32[]{:S(2)}) collective-permute-start(bf16[1280,256]{1,0:T(8,128)(2,1)S(1)} %constant_dynamic-update-slice_fusion.4.refs_0_), channel_id=1, source_target_pairs={{0,64},{4,20},{8,72},{12,28},{16,80},{20,4},{24,88},{28,12},{32,96... | collective-permute-start | bytes 1966088 | tf_op jit(solution)/shard_map/ppermute | solution.py:484
  40.0 3.1 %turn.2.refs_0_.early_ref = bf16[5120,256]{1,0:T(8,128)(2,1)S(1)} custom-call(s32[64]{0:T(128)S(1)} %add.149.offset_ref, bf16[128,5120]{1,0:T(8,128)(2,1)S(1)} %norm.1.first_ref, bf16[128,5120]{1,0:T(8,128)(2,1)} %collective-permute-done.10.second_ref), custom_call_target="tpu_custom_call" | custom-call | tf_op jit(solution)/shard_map/turn/pallas_call | solution.py:226
  43.4 7.1 %collective-permute-done.8.refs_2_ = bf16[1280,256]{1,0:T(8,128)(2,1)S(1)} collective-permute-done((bf16[1280,256]{1,0:T(8,128)(2,1)S(1)}, bf16[1280,256]{1,0:T(8,128)(2,1)S(1)}, u32[]{:S(2)}, u32[]{:S(2)}) %collective-permute-start.8) | collective-permute-done | bytes 655392 | tf_op jit(solution)/shard_map/ppermute | solution.py:484
  61.0 5.4 %collective-permute-start.16 = (bf16[2,128,128]{2,1,0:T(8,128)(2,1)S(1)}, bf16[2,128,128]{2,1,0:T(8,128)(2,1)S(1)}, u32[]{:S(2)}, u32[]{:S(2)}) collective-permute-start(bf16[2,128,128]{2,1,0:T(8,128)(2,1)S(1)} %get-tuple-element.86), channel_id=1, source_target_pairs={{0,132},{1,0},{2,4},{3,128},{4,133},{5,1},{6,5},{7,129},{128,134},... | collective-permute-start | bytes 196616 | tf_op jit(solution)/shard_map/ppermute | solution.py:509
  66.4 3.2 %turn.3.refs_1_.late_ref = bf16[5120,256]{1,0:T(8,128)(2,1)S(1)} custom-call(s32[64]{0:T(128)S(1)} %add.149.offset_ref, bf16[128,5120]{1,0:T(8,128)(2,1)} %collective-permute-done.11.first_ref, bf16[128,5120]{1,0:T(8,128)(2,1)S(1)} %collective-permute-done.12.second_ref), custom_call_target="tpu_custom_call" | custom-call | tf_op jit(solution)/shard_map/turn/pallas_call | solution.py:226
  70.9 5.9 %attention.1 = (bf16[2,128,128]{2,1,0:T(8,128)(2,1)S(1)}, bf16[2,128,128]{2,1,0:T(8,128)(2,1)S(1)}, bf16[2,128,128]{2,1,0:T(8,128)(2,1)S(1)}, bf16[2,128,128]{2,...) custom-call(s32[4]{0:T(128)S(1)} %get-tuple-element.72.order_ref, ...), custom_call_target="tpu_custom_call" | custom-call | tf_op jit(solution)/shard_map/attention/pallas_call | solution.py:346
  78.8 3.7 %collective-permute-start.19 = (bf16[2,128,128]{2,1,0:T(8,128)(2,1)S(1)}, bf16[2,128,128]{2,1,0:T(8,128)(2,1)S(1)}, u32[]{:S(2)}, u32[]{:S(2)}) collective-permute-start(bf16[2,128,128]{2,1,0:T(8,128)(2,1)S(1)} %get-tuple-element.96), channel_id=1, source_target_pairs={{0,2},{1,6},{2,130},{3,134},{4,3},{5,7},{6,131},{7,135},{128,0},{1... | collective-permute-start | bytes 196616 | tf_op jit(solution)/shard_map/ppermute | solution.py:505
  82.5 4.0 %collective-permute-start.20 = (bf16[2,128,128]{2,1,0:T(8,128)(2,1)S(1)}, bf16[2,128,128]{2,1,0:T(8,128)(2,1)S(1)}, u32[]{:S(2)}, u32[]{:S(2)}) collective-permute-start(bf16[2,128,128]{2,1,0:T(8,128)(2,1)S(1)} %get-tuple-element.97), channel_id=1, source_target_pairs={{0,1},{1,5},{2,129},{3,133},{4,2},{5,6},{6,130},{7,134},{128,3},{1... | collective-permute-start | bytes 196616 | tf_op jit(solution)/shard_map/ppermute | solution.py:505
  86.4 3.3 %grad_query.2.refs_0_ = bf16[512,1024]{1,0:T(8,128)(2,1)} custom-call(bf16[512,1024]{1,0:T(8,128)(2,1)S(1)} %copy-done.1, bf16[512,128]{1,0:T(8,128)(2,1)S(1)} %get-tuple-element.91.k_ref, bf16[8,256,512]{2,1,0:T(8,128)(2,1)S(1)} %get-tuple-element.117.ds0_ref, bf16[8,256,256]{2,1,0:T(8,128)(2,1)S(1)} %get-tuple-element.93.ds1_ref, ...), custom_call_target="tpu_custom_call" | custom-call | tf_op jit(solution)/shard_map/grad_query/pallas_call | solution.py:401
  98.8 3.4 %collective-permute-start.22 = (bf16[48,5120]{1,0:T(8,128)(2,1)S(1)}, bf16[48,5120]{1,0:T(8,128)(2,1)S(1)}, u32[]{:S(2)}, u32[]{:S(2)}) collective-permute-start(bf16[48,5120]{1,0:T(8,128)(2,1)S(1)} %get-tuple-element.139), channel_id=1, source_target_pairs={{0,128},{128,0},{1,129},{129,1},{2,130},{130,2},{3,131},{131,3},{4... | collective-permute-start | bytes 1474568 | tf_op jit(solution)/shard_map/ppermute | solution.py:513
  104.1 8.5 %collective-permute-done.22.layer_ref = bf16[48,5120]{1,0:T(8,128)(2,1)S(1)} collective-permute-done((bf16[48,5120]{1,0:T(8,128)(2,1)S(1)}, bf16[48,5120]{1,0:T(8,128)(2,1)S(1)}, u32[]{:S(2)}, u32[]{:S(2)}) %collective-permute-start.22) | collective-permute-done | bytes 491552 | tf_op jit(solution)/shard_map/ppermute | solution.py:513
  114.1 3.2 %collective-permute-start.27 = (bf16[320,256]{1,0:T(8,128)(2,1)S(1)}, bf16[320,256]{1,0:T(8,128)(2,1)S(1)}, u32[]{:S(2)}, u32[]{:S(2)}) collective-permute-start(bf16[320,256]{1,0:T(8,128)(2,1)S(1)} %get-tuple-element.114), channel_id=1, source_target_pairs={{0,24},{4,100},{8,0},{12,108},{16,8},{20,116},{24,16},{28,124},{32... | collective-permute-start | bytes 491528 | tf_op jit(solution)/shard_map/ppermute | solution.py:488
  119.0 3.3 %grad_query.3 = bf16[512,1024]{1,0:T(8,128)(2,1)} custom-call(bf16[512,1024]{1,0:T(8,128)(2,1)S(1)} %copy-done.1, bf16[512,128]{1,0:T(8,128)(2,1)S(1)} %get-tuple-element.91.k_ref, bf16[8,256,512]{2,1,0:T(8,128)(2,1)S(1)} %get-tuple-element.117.ds0_ref, bf16[8,256,256]{2,1,0:T(8,128)(2,1)S(1)} %get-tuple-element.93.ds1_ref, ...), custom_call_target="tpu_custom_call", output_to_operand_aliasing={{}: (6, {})} | custom-call | tf_op jit(solution)/shard_map/grad_query/pallas_call | solution.py:401
  124.8 5.3 %collective-permute-start.30 = (bf16[80,256]{1,0:T(8,128)(2,1)S(1)}, bf16[80,256]{1,0:T(8,128)(2,1)S(1)}, u32[]{:S(2)}, u32[]{:S(2)}) collective-permute-start(bf16[80,256]{1,0:T(8,128)(2,1)S(1)} %get-tuple-element.122), channel_id=1, source_target_pairs={{0,0},{1,4},{2,128},{3,132},{4,1},{5,5},{6,129},{7,133},{128,2},{1... | collective-permute-start | bytes 122888 | tf_op jit(solution)/shard_map/ppermute | solution.py:509
  130.1 3.0 %collective-permute-start.31 = (bf16[80,256]{1,0:T(8,128)(2,1)S(1)}, bf16[80,256]{1,0:T(8,128)(2,1)S(1)}, u32[]{:S(2)}, u32[]{:S(2)}) collective-permute-start(bf16[80,256]{1,0:T(8,128)(2,1)S(1)} %get-tuple-element.123), channel_id=1, source_target_pairs={{0,132},{1,0},{2,4},{3,128},{4,133},{5,1},{6,5},{7,129},{128,134},... | collective-permute-start | bytes 122888 | tf_op jit(solution)/shard_map/ppermute | solution.py:509
  133.1 3.7 %collective-permute-start.32 = (bf16[80,256]{1,0:T(8,128)(2,1)S(1)}, bf16[80,256]{1,0:T(8,128)(2,1)S(1)}, u32[]{:S(2)}, u32[]{:S(2)}) collective-permute-start(bf16[80,256]{1,0:T(8,128)(2,1)S(1)} %get-tuple-element.124), channel_id=1, source_target_pairs={{0,128},{1,132},{2,0},{3,4},{4,129},{5,133},{6,1},{7,5},{128,130},... | collective-permute-start | bytes 122888 | tf_op jit(solution)/shard_map/ppermute | solution.py:509
  136.9 2.7 %grad_tokens.3.refs_0_ = bf16[128,5120]{1,0:T(8,128)(2,1)} custom-call(bf16[128,5120]{1,0:T(8,128)(2,1)} %x_ref.5, bf16[128,5120]{1,0:T(8,128)(2,1)} %add_convert_fusion.mine_ref, bf16[48,5120]{1,0:T(8,128)(2,1)} %copy-done.3), custom_call_target="tpu_custom_call" | custom-call | tf_op jit(solution)/shard_map/grad_tokens/pallas_call | solution.py:459
  139.7 3.4 %collective-permute-start.34 = (bf16[32,5120]{1,0:T(8,128)(2,1)S(1)}, bf16[32,5120]{1,0:T(8,128)(2,1)S(1)}, u32[]{:S(2)}, u32[]{:S(2)}) collective-permute-start(bf16[32,5120]{1,0:T(8,128)(2,1)S(1)} %slice.70), channel_id=1, source_target_pairs={{0,128},{128,0},{1,129},{129,1},{2,130},{130,2},{3,131},{131,3},{4... | collective-permute-start | bytes 983048 | tf_op jit(solution)/shard_map/ppermute | solution.py:513
  144.8 7.5 %all-to-all-start = ((bf16[64,2,160]{2,1,0:T(2,128)(2,1)}), bf16[64,2,160]{2,1,0:T(2,128)(2,1)S(1)}, u32[]{:S(2)}, u32[]{:S(2)}) async-start(bf16[64,2,160]{2,1,0:T(2,128)(2,1)} %copy.21), calls=%async_computation | async-start | bytes 131072 | tf_op jit(solution)/shard_map/all_to_all | solution.py:640
  152.3 2.8 %grad_tokens.4.refs_0_ = bf16[128,5120]{1,0:T(8,128)(2,1)} custom-call(bf16[128,5120]{1,0:T(8,128)(2,1)} %x_ref.5, bf16[128,5120]{1,0:T(8,128)(2,1)} %add_convert_fusion.mine_ref, bf16[48,5120]{1,0:T(8,128)(2,1)} %copy-done.4, bf16[128,5120]{1,0:T(8,128)(2,1)} %grad_tokens.3.refs_0_), custom_call_target="tpu_custom_call", output_to_operand_aliasing={{}: (3, {})} | custom-call | tf_op jit(solution)/shard_map/grad_tokens/pallas_call | solution.py:459
  (120 shorter events, 57.8 us)
Async XLA Ops:
  1.6 20.4 %collective-permute-start.3 = (bf16[80,256]{1,0:T(8,128)(2,1)S(1)}, bf16[80,256]{1,0:T(8,128)(2,1)S(1)}, u32[]{:S(2)}, u32[]{:S(2)}) collective-permute-start(bf16[80,256]{1,0:T(8,128)(2,1)S(1)} %pad_maximum_fusion.4), channel_id=1, source_target_pairs={{0,3},{1,7},{2,131},{3,135},{4,0},{5,4},{6,128},{7,132},{128,1},{1... | collective-permute-start | bytes 122888 | tf_op jit(solution)/shard_map/ppermute | solution.py:505
  4.9 17.1 %collective-permute-start.2 = (bf16[80,256]{1,0:T(8,128)(2,1)S(1)}, bf16[80,256]{1,0:T(8,128)(2,1)S(1)}, u32[]{:S(2)}, u32[]{:S(2)}) collective-permute-start(bf16[80,256]{1,0:T(8,128)(2,1)S(1)} %pad_maximum_fusion.4), channel_id=1, source_target_pairs={{0,2},{1,6},{2,130},{3,134},{4,3},{5,7},{6,131},{7,135},{128,0},{1... | collective-permute-start | bytes 122888 | tf_op jit(solution)/shard_map/ppermute | solution.py:505
  9.5 12.4 %collective-permute-start.1 = (bf16[80,256]{1,0:T(8,128)(2,1)S(1)}, bf16[80,256]{1,0:T(8,128)(2,1)S(1)}, u32[]{:S(2)}, u32[]{:S(2)}) collective-permute-start(bf16[80,256]{1,0:T(8,128)(2,1)S(1)} %pad_maximum_fusion.4), channel_id=1, source_target_pairs={{0,1},{1,5},{2,129},{3,133},{4,2},{5,6},{6,130},{7,134},{128,3},{1... | collective-permute-start | bytes 122888 | tf_op jit(solution)/shard_map/ppermute | solution.py:505
  16.4 23.6 %collective-permute-start.10 = (bf16[128,5120]{1,0:T(8,128)(2,1)S(1)}, bf16[128,5120]{1,0:T(8,128)(2,1)}, u32[]{:S(2)}, u32[]{:S(2)}) collective-permute-start(bf16[128,5120]{1,0:T(8,128)(2,1)S(1)} %norm.1.first_ref), channel_id=1, source_target_pairs={{0,4},{4,0},{1,5},{5,1},{2,6},{6,2},{3,7},{7,3},{8,12},{12,8},{9,1... | collective-permute-start | bytes 3932168 | tf_op jit(solution)/shard_map/ppermute | solution.py:492
  18.1 32.4 %collective-permute-start.11 = (bf16[128,5120]{1,0:T(8,128)(2,1)S(1)}, bf16[128,5120]{1,0:T(8,128)(2,1)}, u32[]{:S(2)}, u32[]{:S(2)}) collective-permute-start(bf16[128,5120]{1,0:T(8,128)(2,1)S(1)} %norm.1.first_ref), channel_id=1, source_target_pairs={{0,128},{128,0},{1,129},{129,1},{2,130},{130,2},{3,131},{131,3},{4... | collective-permute-start | bytes 3932168 | tf_op jit(solution)/shard_map/ppermute | solution.py:513
  22.0 10.0 %collective-permute-start.5 = (bf16[320,256]{1,0:T(8,128)(2,1)S(1)}, bf16[320,256]{1,0:T(8,128)(2,1)S(1)}, u32[]{:S(2)}, u32[]{:S(2)}) collective-permute-start(bf16[320,256]{1,0:T(8,128)(2,1)S(1)} %get-tuple-element.146), channel_id=1, source_target_pairs={{0,24},{4,100},{8,0},{12,108},{16,8},{20,116},{24,16},{28,124},{32... | collective-permute-start | bytes 491528 | tf_op jit(solution)/shard_map/ppermute | solution.py:488
  32.1 11.4 %collective-permute-start.9 = (bf16[1280,256]{1,0:T(8,128)(2,1)S(1)}, bf16[1280,256]{1,0:T(8,128)(2,1)S(1)}, u32[]{:S(2)}, u32[]{:S(2)}) collective-permute-start(bf16[1280,256]{1,0:T(8,128)(2,1)S(1)} %constant_dynamic-update-slice_fusion.4.refs_0_), channel_id=1, source_target_pairs={{0,64},{4,20},{8,72},{12,28},{16,80},{20,4},{24,88},{28,12},{32,96... | collective-permute-start | bytes 1966088 | tf_op jit(solution)/shard_map/ppermute | solution.py:484
  34.8 15.7 %collective-permute-start.8 = (bf16[1280,256]{1,0:T(8,128)(2,1)S(1)}, bf16[1280,256]{1,0:T(8,128)(2,1)S(1)}, u32[]{:S(2)}, u32[]{:S(2)}) collective-permute-start(bf16[1280,256]{1,0:T(8,128)(2,1)S(1)} %constant_dynamic-update-slice_fusion.4.refs_0_), channel_id=1, source_target_pairs={{0,96},{4,28},{8,104},{12,4},{16,112},{20,12},{24,120},{28,20},{32... | collective-permute-start | bytes 1966088 | tf_op jit(solution)/shard_map/ppermute | solution.py:484
  35.6 15.0 %collective-permute-start.7 = (bf16[1280,256]{1,0:T(8,128)(2,1)S(1)}, bf16[1280,256]{1,0:T(8,128)(2,1)S(1)}, u32[]{:S(2)}, u32[]{:S(2)}) collective-permute-start(bf16[1280,256]{1,0:T(8,128)(2,1)S(1)} %constant_dynamic-update-slice_fusion.4.refs_0_), channel_id=1, source_target_pairs={{0,32},{4,12},{8,40},{12,20},{16,48},{20,28},{24,56},{28,4},{32,64... | collective-permute-start | bytes 1966088 | tf_op jit(solution)/shard_map/ppermute | solution.py:484
  57.1 12.5 %collective-permute-start.13 = (bf16[2,128,128]{2,1,0:T(8,128)(2,1)S(1)}, bf16[2,128,128]{2,1,0:T(8,128)(2,1)S(1)}, u32[]{:S(2)}, u32[]{:S(2)}) collective-permute-start(bf16[2,128,128]{2,1,0:T(8,128)(2,1)S(1)} %get-tuple-element.83), channel_id=1, source_target_pairs={{0,0},{1,4},{2,128},{3,132},{4,1},{5,5},{6,129},{7,133},{128,2},{1... | collective-permute-start | bytes 196616 | tf_op jit(solution)/shard_map/ppermute | solution.py:509
  59.0 10.6 %collective-permute-start.14 = (bf16[2,128,128]{2,1,0:T(8,128)(2,1)S(1)}, bf16[2,128,128]{2,1,0:T(8,128)(2,1)S(1)}, u32[]{:S(2)}, u32[]{:S(2)}) collective-permute-start(bf16[2,128,128]{2,1,0:T(8,128)(2,1)S(1)} %get-tuple-element.84), channel_id=1, source_target_pairs={{0,4},{1,128},{2,132},{3,0},{4,5},{5,129},{6,133},{7,1},{128,6},{1... | collective-permute-start | bytes 196616 | tf_op jit(solution)/shard_map/ppermute | solution.py:509
  59.3 10.3 %collective-permute-start.15 = (bf16[2,128,128]{2,1,0:T(8,128)(2,1)S(1)}, bf16[2,128,128]{2,1,0:T(8,128)(2,1)S(1)}, u32[]{:S(2)}, u32[]{:S(2)}) collective-permute-start(bf16[2,128,128]{2,1,0:T(8,128)(2,1)S(1)} %get-tuple-element.85), channel_id=1, source_target_pairs={{0,128},{1,132},{2,0},{3,4},{4,129},{5,133},{6,1},{7,5},{128,130},... | collective-permute-start | bytes 196616 | tf_op jit(solution)/shard_map/ppermute | solution.py:509
  61.0 9.9 %collective-permute-start.16 = (bf16[2,128,128]{2,1,0:T(8,128)(2,1)S(1)}, bf16[2,128,128]{2,1,0:T(8,128)(2,1)S(1)}, u32[]{:S(2)}, u32[]{:S(2)}) collective-permute-start(bf16[2,128,128]{2,1,0:T(8,128)(2,1)S(1)} %get-tuple-element.86), channel_id=1, source_target_pairs={{0,132},{1,0},{2,4},{3,128},{4,133},{5,1},{6,5},{7,129},{128,134},... | collective-permute-start | bytes 196616 | tf_op jit(solution)/shard_map/ppermute | solution.py:509
  76.8 12.9 %collective-permute-start.17 = (bf16[2,128,128]{2,1,0:T(8,128)(2,1)S(1)}, bf16[2,128,128]{2,1,0:T(8,128)(2,1)S(1)}, u32[]{:S(2)}, u32[]{:S(2)}) collective-permute-start(bf16[2,128,128]{2,1,0:T(8,128)(2,1)S(1)} %get-tuple-element.94), channel_id=1, source_target_pairs={{0,0},{1,4},{2,128},{3,132},{4,1},{5,5},{6,129},{7,133},{128,2},{1... | collective-permute-start | bytes 196616 | tf_op jit(solution)/shard_map/ppermute | solution.py:505
  78.7 11.0 %collective-permute-start.18 = (bf16[2,128,128]{2,1,0:T(8,128)(2,1)S(1)}, bf16[2,128,128]{2,1,0:T(8,128)(2,1)S(1)}, u32[]{:S(2)}, u32[]{:S(2)}) collective-permute-start(bf16[2,128,128]{2,1,0:T(8,128)(2,1)S(1)} %get-tuple-element.95), channel_id=1, source_target_pairs={{0,3},{1,7},{2,131},{3,135},{4,0},{5,4},{6,128},{7,132},{128,1},{1... | collective-permute-start | bytes 196616 | tf_op jit(solution)/shard_map/ppermute | solution.py:505
  78.8 10.9 %collective-permute-start.19 = (bf16[2,128,128]{2,1,0:T(8,128)(2,1)S(1)}, bf16[2,128,128]{2,1,0:T(8,128)(2,1)S(1)}, u32[]{:S(2)}, u32[]{:S(2)}) collective-permute-start(bf16[2,128,128]{2,1,0:T(8,128)(2,1)S(1)} %get-tuple-element.96), channel_id=1, source_target_pairs={{0,2},{1,6},{2,130},{3,134},{4,3},{5,7},{6,131},{7,135},{128,0},{1... | collective-permute-start | bytes 196616 | tf_op jit(solution)/shard_map/ppermute | solution.py:505
  93.9 19.8 %collective-permute-start.24 = (bf16[1280,256]{1,0:T(8,128)(2,1)S(1)}, bf16[1280,256]{1,0:T(8,128)(2,1)S(1)}, u32[]{:S(2)}, u32[]{:S(2)}) collective-permute-start(bf16[1280,256]{1,0:T(8,128)(2,1)S(1)} %get-tuple-element.102), channel_id=1, source_target_pairs={{0,96},{4,28},{8,104},{12,4},{16,112},{20,12},{24,120},{28,20},{32... | collective-permute-start | bytes 1966088 | tf_op jit(solution)/shard_map/ppermute | solution.py:484
  94.9 18.8 %collective-permute-start.25 = (bf16[1280,256]{1,0:T(8,128)(2,1)S(1)}, bf16[1280,256]{1,0:T(8,128)(2,1)S(1)}, u32[]{:S(2)}, u32[]{:S(2)}) collective-permute-start(bf16[1280,256]{1,0:T(8,128)(2,1)S(1)} %get-tuple-element.111), channel_id=1, source_target_pairs={{0,32},{4,12},{8,40},{12,20},{16,48},{20,28},{24,56},{28,4},{32,64... | collective-permute-start | bytes 1966088 | tf_op jit(solution)/shard_map/ppermute | solution.py:484
  95.3 18.4 %collective-permute-start.26 = (bf16[1280,256]{1,0:T(8,128)(2,1)S(1)}, bf16[1280,256]{1,0:T(8,128)(2,1)S(1)}, u32[]{:S(2)}, u32[]{:S(2)}) collective-permute-start(bf16[1280,256]{1,0:T(8,128)(2,1)S(1)} %get-tuple-element.112), channel_id=1, source_target_pairs={{0,64},{4,20},{8,72},{12,28},{16,80},{20,4},{24,88},{28,12},{32,96... | collective-permute-start | bytes 1966088 | tf_op jit(solution)/shard_map/ppermute | solution.py:484
  98.8 13.8 %collective-permute-start.22 = (bf16[48,5120]{1,0:T(8,128)(2,1)S(1)}, bf16[48,5120]{1,0:T(8,128)(2,1)S(1)}, u32[]{:S(2)}, u32[]{:S(2)}) collective-permute-start(bf16[48,5120]{1,0:T(8,128)(2,1)S(1)} %get-tuple-element.139), channel_id=1, source_target_pairs={{0,128},{128,0},{1,129},{129,1},{2,130},{130,2},{3,131},{131,3},{4... | collective-permute-start | bytes 1474568 | tf_op jit(solution)/shard_map/ppermute | solution.py:513
  112.6 12.3 %collective-permute-start.23 = (bf16[48,5120]{1,0:T(8,128)(2,1)S(1)}, bf16[48,5120]{1,0:T(8,128)(2,1)S(1)}, u32[]{:S(2)}, u32[]{:S(2)}) collective-permute-start(bf16[48,5120]{1,0:T(8,128)(2,1)S(1)} %get-tuple-element.109), channel_id=1, source_target_pairs={{0,128},{128,0},{1,129},{129,1},{2,130},{130,2},{3,131},{131,3},{4... | collective-permute-start | bytes 1474568 | tf_op jit(solution)/shard_map/ppermute | solution.py:513
  124.8 14.8 %collective-permute-start.30 = (bf16[80,256]{1,0:T(8,128)(2,1)S(1)}, bf16[80,256]{1,0:T(8,128)(2,1)S(1)}, u32[]{:S(2)}, u32[]{:S(2)}) collective-permute-start(bf16[80,256]{1,0:T(8,128)(2,1)S(1)} %get-tuple-element.122), channel_id=1, source_target_pairs={{0,0},{1,4},{2,128},{3,132},{4,1},{5,5},{6,129},{7,133},{128,2},{1... | collective-permute-start | bytes 122888 | tf_op jit(solution)/shard_map/ppermute | solution.py:509
  139.7 15.4 %collective-permute-start.34 = (bf16[32,5120]{1,0:T(8,128)(2,1)S(1)}, bf16[32,5120]{1,0:T(8,128)(2,1)S(1)}, u32[]{:S(2)}, u32[]{:S(2)}) collective-permute-start(bf16[32,5120]{1,0:T(8,128)(2,1)S(1)} %slice.70), channel_id=1, source_target_pairs={{0,128},{128,0},{1,129},{129,1},{2,130},{130,2},{3,131},{131,3},{4... | collective-permute-start | bytes 983048 | tf_op jit(solution)/shard_map/ppermute | solution.py:513
  144.8 15.6 %all-to-all-start = ((bf16[64,2,160]{2,1,0:T(2,128)(2,1)}), bf16[64,2,160]{2,1,0:T(2,128)(2,1)S(1)}, u32[]{:S(2)}, u32[]{:S(2)}) async-start(bf16[64,2,160]{2,1,0:T(2,128)(2,1)} %copy.21), calls=%async_computation | async-start | bytes 131072 | tf_op jit(solution)/shard_map/all_to_all | solution.py:640
  (23 other events, 220.5 us)
